TPU v7x, 512 devices: a whole 4x4x16 slice. The times are simulated.
512 devices in a mesh: seq: 64 (over y, z), fsdp: 8 (over x, core).
Axes of the slice: x: 4, y: 4, z: 16, core: 2. Of those that a mesh axis runs over, the one named last changes fastest.
Arguments:
- hidden: bfloat16 [8, 8192, 5120], P('fsdp', 'seq'), may hold values from -6 to 6
- inputs: bfloat16 [8, 8192, 2048], P('fsdp', 'seq'), may hold values from -6 to 6
- w_b: bfloat16 [5120, 128], P('fsdp'), may hold values from -0.078125 to 0.078125
- conv_x: float32 [4, 2048], replicated, may hold values from -3 to 3
- conv_b: float32 [4, 128], replicated, may hold values from -3 to 3
- log_decay: float32 [8, 8192, 64], P('fsdp', 'seq'), may hold values from -3.5 to 0, as said below
- accepted: int32 [8, 64], P('fsdp', 'seq'), may hold values from 0 to 128, as said below
Outputs:
- accepted_states: float32 [8, 64, 64, 32, 128], P('fsdp', 'seq')
Inputs may be any that keep to these rules, and one draw needn't show every extreme that they name: `log_decay`: every entry is negative. `accepted`: in every context some shard keeps all 128 tokens.
All inputs are finite; a program needn't handle non-finite values.
Results may differ from a plain program's by a relative error of at most 0.0003.
Values may be sent and summed in bfloat16 or wider, within the bound.
No kernel may reach another device: no remote copies, remote signals or barrier semaphores. Data moves between devices by JAX's collectives and lax.ppermute only.
A program may use at most 192 MiB of HBM per device.

v0:
```python
import jax
import jax.numpy as jnp
from jax import lax
from jax.sharding import PartitionSpec as P


def passed_along(value, axis, by):
    devices = lax.axis_size(axis)
    pairs = [(i, i + by) for i in range(devices) if 0 <= i + by < devices]
    return lax.ppermute(value, axis, pairs)


def carried_in(part, axis, combine, identity):
    place = lax.axis_index(axis)
    gathered = jax.tree.map(lambda a: lax.all_gather(a, axis), part)
    state = jax.tree.map(lambda a, e: jnp.zeros_like(a) + jnp.asarray(e, a.dtype), part, identity)

    def one(lap, state):
        return combine(
            state, jax.tree.map(lambda a: lax.dynamic_index_in_dim(a, lap, 0, False), gathered)
        )

    return lax.fori_loop(0, place, one, state)


def conv_rows(extended, weight):
    kernel = weight.shape[0]
    length = extended.shape[0] - kernel + 1
    summed = jnp.zeros((length, extended.shape[1]), jnp.float32)
    for offset in range(kernel):
        summed = summed + weight[offset] * extended[offset : offset + length]
    return jax.nn.silu(summed)


def shard_states(flat_x, mixed_b, log_step, accepted, headdim):
    length = log_step.shape[0]
    head_count = log_step.shape[1]
    state_size = mixed_b.shape[1]
    prefix = jnp.concatenate(
        [jnp.zeros((1, head_count), jnp.float32), jnp.cumsum(log_step, axis=0)], 0
    )
    end_logs = prefix[length]
    chosen = (jnp.arange(length + 1) == accepted).astype(jnp.float32)
    kept_log = jnp.sum(chosen[:, None] * prefix, axis=0)
    after_log = prefix[1:]
    inside = (jnp.arange(length) < accepted)[:, None]
    weight_end = jnp.exp(end_logs[None, :] - after_log)
    weight_kept = jnp.where(
        inside, jnp.exp(jnp.where(inside, kept_log[None, :] - after_log, 0.0)), 0.0
    )
    wide_end = jnp.repeat(weight_end, headdim, axis=1)
    wide_kept = jnp.repeat(weight_kept, headdim, axis=1)
    full_state = jnp.einsum(
        "tc,tn->cn", wide_end * flat_x, mixed_b, precision=lax.Precision.HIGHEST
    )
    kept_state = jnp.einsum(
        "tc,tn->cn", wide_kept * flat_x, mixed_b, precision=lax.Precision.HIGHEST
    )
    full_state = full_state.reshape(head_count, headdim, state_size)
    kept_state = kept_state.reshape(head_count, headdim, state_size)
    return (end_logs, kept_log, full_state, kept_state)


def link_states(earlier, later):
    return (earlier[0] + later[0], jnp.exp(later[0])[:, None, None] * earlier[1] + later[1])


def on_device(hidden, inputs, w_b, conv_x, conv_b, log_decay, accepted):
    tokens = hidden[0]
    values = inputs[0]
    length = tokens.shape[0]
    margin = conv_x.shape[0] - 1
    head_count = log_decay.shape[2]
    headdim = values.shape[1] // head_count
    state_size = w_b.shape[1]
    before = passed_along(values[length - margin :], "seq", 1)
    values_extended = jnp.concatenate([before, values], 0)
    projected = jnp.dot(
        tokens, lax.all_gather(w_b, "fsdp", axis=0, tiled=True), preferred_element_type=jnp.float32
    )
    b_before = passed_along(projected[length - margin :], "seq", 1)
    b_extended = jnp.concatenate([b_before, projected], 0)
    flat_x = conv_rows(values_extended.astype(jnp.float32), conv_x)
    mixed_b = conv_rows(b_extended, conv_b)
    end_logs, kept_log, full_state, kept_state = shard_states(
        flat_x, mixed_b, log_decay[0], accepted[0, 0], headdim
    )
    zero_logs = jnp.zeros_like(end_logs)
    zero_states = jnp.zeros_like(full_state)
    scanned = carried_in((end_logs, full_state), "seq", link_states, (zero_logs, zero_states))
    incoming = scanned[1]
    final = jnp.exp(kept_log)[:, None, None] * incoming + kept_state
    return final.reshape(1, 1, head_count, headdim, state_size)


def solution(mesh):
    placed = (
        P("fsdp", "seq", None),
        P("fsdp", "seq", None),
        P("fsdp", None),
        P(),
        P(),
        P("fsdp", "seq", None),
        P("fsdp", "seq"),
    )
    return jax.shard_map(
        on_device,
        mesh=mesh,
        in_specs=placed,
        out_specs=P("fsdp", "seq", None, None, None),
        check_vma=False,
    )
```

profile of v0, /device:TPU:504, one launch (start us, length us, event | category | flops | bytes accessed | tf_op | source)
XLA Modules:
  0.0 662.4 jit_solution(2036156475693223328)
XLA Ops:
  11.4 28.5 %all-gather.4.cloned.1.call-done = bf16[5120,128]{1,0:T(8,128)(2,1)} async-done(((bf16[640,128]{1,0:T(8,128)(2,1)}), bf16[5120,128]{1,0:T(8,128)(2,1)}) %all-gather.4.cloned.1.call-update) | async-done | bytes 1310736 | tf_op jit(solution)/shard_map/all_gather | solution.py:79
  40.0 1.8 fusion
  43.5 2.3 bitcast_multiply_fusion.1
  47.4 1.9 fusion.14
  49.4 73.3 %all-gather = f32[64,1,64]{2,1,0:T(1,128)S(1)} all-gather(f32[1,1,64]{2,1,0:T(1,128)S(1)} %get-tuple-element.62), channel_id=1, replica_groups=mesh['seq'=64,'fsdp'=8] {'seq'}, dimensions={0}, use_global_device_ids=true | all-gather | bytes 16640 | tf_op jit(solution)/shard_map/all_gather | solution.py:15
  123.7 436.3 %all-gather.6.cloned.1.call-done = f32[64,64,32,128]{3,2,1,0:T(8,128)} async-done(((f32[1,64,32,128]{3,2,1,0:T(8,128)}), f32[64,64,32,128]{3,2,1,0:T(8,128)}) %all-gather.6.cloned.1.call-update) | async-done | bytes 67108880 | tf_op jit(solution)/shard_map/all_gather | solution.py:15
  560.2 94.2 %while.12 = (s32[]{:T(128)}, f32[64,32,128]{2,1,0:T(8,128)S(1)}, s32[]{:T(128)}, f32[64,64]{1,0:T(8,128)S(1)}, f32[64,64,32,128]{3,2,1,0:T(8,128)}, /*index=5*/s32[]{:T(128)}, s32[]{:T(128)}, s32[]{:T(128)}) while((s32[]{:T(128)}, f32[64,32,128]{2,1,0:T(8,128)S(1)}, s32[]{:T(128)}, f32[64,64]{1,0:T(8,128)S(1)}, f32[64,64,32,128]{3,2,1,0:T(8,128)}, ...), condition=%wide.region_3.4_spmd, body=%wide.region_2.3_spmd.sunk | while | flops 524293 | bytes 3146631 | solution.py:23
  560.2 1.4 bitcast_add_fusion.2
  561.7 1.4 bitcast_add_fusion.2
  563.2 1.4 bitcast_add_fusion.2
  564.7 1.4 bitcast_add_fusion.2
  566.2 1.4 bitcast_add_fusion.2
  567.7 1.4 bitcast_add_fusion.2
  569.2 1.4 bitcast_add_fusion.2
  570.7 1.4 bitcast_add_fusion.2
  572.2 1.4 bitcast_add_fusion.2
  573.7 1.4 bitcast_add_fusion.2
  575.2 1.4 bitcast_add_fusion.2
  576.7 1.4 bitcast_add_fusion.2
  578.2 1.4 bitcast_add_fusion.2
  579.6 1.4 bitcast_add_fusion.2
  581.1 1.4 bitcast_add_fusion.2
  582.6 1.4 bitcast_add_fusion.2
  584.1 1.4 bitcast_add_fusion.2
  585.6 1.4 bitcast_add_fusion.2
  587.1 1.4 bitcast_add_fusion.2
  588.6 1.4 bitcast_add_fusion.2
  596.1 1.4 bitcast_add_fusion.2
  615.5 1.4 bitcast_add_fusion.2
  624.5 1.4 bitcast_add_fusion.2
  643.9 1.4 bitcast_add_fusion.2
  652.9 1.4 bitcast_add_fusion.2
  (138 shorter events, 65.6 us)
Async XLA Ops:
  6.5 33.5 %copy-start = (bf16[1,128,5120]{2,1,0:T(8,128)(2,1)S(1)}, bf16[1,128,5120]{2,1,0:T(8,128)(2,1)}, u32[]{:S(2)}) copy-start(bf16[1,128,5120]{2,1,0:T(8,128)(2,1)} %param.9) | copy-start | bytes 3932164
  6.5 4.3 copy-start.1
  6.5 4.8 copy-start.3
  6.5 4.9 copy-start.2
  6.5 33.4 %all-gather.4.cloned.1.call-start = ((), (), s32[]{:S(2)}) async-start(), calls=%async_computation | async-start | bytes 1474560 | tf_op jit(solution)/shard_map/all_gather | solution.py:79
  7.3 552.8 %all-gather.6.cloned.1.call-start = ((), (), s32[]{:S(2)}) async-start(), calls=%async_computation.1 | async-start | bytes 68157440 | tf_op jit(solution)/shard_map/all_gather | solution.py:15
  8.8 34.3 %collective-permute-start = (bf16[3,2048]{0,1:T(8,128)(2,1)S(1)}, bf16[3,2048]{0,1:T(8,128)(2,1)S(1)}, u32[]{:S(2)}, u32[]{:S(2)}) collective-permute-start(bf16[3,2048]{0,1:T(8,128)(2,1)S(1)} %slice_bitcast_fusion), channel_id=1, source_target_pairs={{0,8},{8,16},{16,24},{24,32},{32,40},{40,48},{48,56},{56,64},{64,7... | collective-permute-start | bytes 36872 | tf_op jit(solution)/shard_map/ppermute | solution.py:10
  41.8 5.5 collective-permute-start.1
Sparse Core Ops, SparseCore 0:
  9.5 30.4 all-gather.3
  49.4 510.5 all-gather.5
where the time goes:
time: 665 us; the launch traced here: 662 us
  waiting for transfers between devices  467 us (70%)
  other arithmetic  95.6 us (14%)
  blocking collectives  73.3 us (11%)
  between operations  14.2 us (2%)
    all_gather x1, waiting for transfers between devices, carried_in(): gathered = jax.tree.map(lambda a: lax.all_gather(a, axis), part)  436 us
    add x63, other arithmetic, link_states(): jnp.exp(later[0])[:, None, None] * earlier[1] + later[1]  91.2 us
    all_gather x1, blocking collectives, carried_in(): gathered = jax.tree.map(lambda a: lax.all_gather(a, axis), part)  73.3 us
    all_gather x1, waiting for transfers between devices, on_device(): lax.all_gather(w_b, 'fsdp', axis=0, tiled=True)  28.5 us
  transfers between devices with their start and end apart: 4, of which 3 were waited for; matrix products, arithmetic and copies ran while one was open for 1% of the time, Pallas kernels for 0%

commit v1 on v0

v1 whole, which is shorter than its diff:
```python
import functools

import jax
import jax.numpy as jnp
from jax import lax
from jax.experimental import pallas as pl
from jax.experimental.pallas import tpu as pltpu
from jax.sharding import PartitionSpec as P

GROUP = 4
ROWS = 16
TOP = 32760.0
FINE = 128.0
LOG_STEP = float(2**19)
VMEM = 48 * 1024 * 1024

call = functools.partial(
    pl.pallas_call, compiler_params=pltpu.CompilerParams(vmem_limit_bytes=VMEM)
)


def code_states(states):
    top = jnp.maximum(jnp.max(jnp.abs(states), axis=1), 1e-33)
    scale = jnp.ceil(jnp.log2(top) * FINE)
    codes = states * (TOP * jnp.exp2(scale * (-1.0 / FINE)))[:, None, :]
    codes = jnp.round(codes).astype(jnp.int32).astype(jnp.int16)
    return codes, scale.astype(jnp.int32).astype(jnp.int16)


def read_states(codes, scale):
    step = jnp.exp2(scale.astype(jnp.int32).astype(jnp.float32) * (1.0 / FINE)) * (1.0 / TOP)
    return codes.astype(jnp.int32).astype(jnp.float32) * step[:, None, :]


def code_logs(logs):
    whole = jnp.round(logs * -LOG_STEP).astype(jnp.int32)
    high = lax.shift_right_logical(whole, 15)
    return high.astype(jnp.int16), (whole - high * 32768).astype(jnp.int16)


def read_logs(high, low):
    whole = high.astype(jnp.int32) * 32768 + low.astype(jnp.int32)
    return whole.astype(jnp.float32) * (-1.0 / LOG_STEP)


def partial_kernel(place, hidden, tail, w0, w1, w2, w3, total):
    depth = w0.shape[0]
    main = jnp.zeros((hidden.shape[0], w0.shape[1]), jnp.float32)
    edge = jnp.zeros((tail.shape[0], w0.shape[1]), jnp.float32)
    for step, w in enumerate((w0, w1, w2, w3)):
        owner = place[1] ^ (2 * step)
        columns = pl.ds(pl.multiple_of(owner * depth, 128), depth)
        main += jnp.dot(hidden[:, columns], w[...], preferred_element_type=jnp.float32)
        edge += jnp.dot(tail[:, columns], w[...], preferred_element_type=jnp.float32)
    total[0:ROWS, :] = edge
    total[ROWS:, :] = main


def mixed_b_kernel(place, hidden, tail, w, taps, begun, mixed, extended):
    depth = w.shape[1]
    main = begun[ROWS:, :]
    edge = begun[0:ROWS, :]
    for step in range(GROUP):
        owner = place[1] ^ (2 * step + 1)
        columns = pl.ds(pl.multiple_of(owner * depth, 128), depth)
        main += jnp.dot(hidden[:, columns], w[step], preferred_element_type=jnp.float32)
        edge += jnp.dot(tail[:, columns], w[step], preferred_element_type=jnp.float32)
    extended[0:ROWS, :] = edge
    extended[ROWS:, :] = main
    kernel = taps.shape[0]
    length = mixed.shape[0]
    summed = jnp.zeros(mixed.shape, jnp.float32)
    for offset in range(kernel):
        first = ROWS - kernel + 1 + offset
        summed = summed + taps[offset : offset + 1, :] * extended[first : first + length, :]
    mixed[...] = summed * jax.nn.sigmoid(summed)


def split_lanes(wide):
    high = wide.astype(jnp.bfloat16)
    low = (wide - high.astype(jnp.float32)).astype(jnp.bfloat16)
    return jnp.concatenate([high, low], axis=1)


def mixed_x_kernel(values, tail, taps, weight_end, weight_kept, ends, kepts, extended):
    length = values.shape[0]
    kernel = taps.shape[0]
    extended[0:ROWS, :] = tail[...].astype(jnp.float32)
    extended[ROWS:, :] = values[...].astype(jnp.float32)
    summed = jnp.zeros(values.shape, jnp.float32)
    for offset in range(kernel):
        first = ROWS - kernel + 1 + offset
        summed = summed + taps[offset : offset + 1, :] * extended[first : first + length, :]
    mixed = (summed * jax.nn.sigmoid(summed)).T
    heads = weight_end.shape[0]
    mixed = mixed.reshape(heads, mixed.shape[0] // heads, length)
    for weight, out in ((weight_end, ends), (weight_kept, kepts)):
        out[...] = split_lanes((mixed * weight[...][:, None, :]).reshape(-1, length))


def state_of(sides, mixed_b):
    high = mixed_b.astype(jnp.bfloat16)
    low = (mixed_b - high.astype(jnp.float32)).astype(jnp.bfloat16)
    size = mixed_b.shape[1]
    right = jnp.concatenate(
        [
            jnp.concatenate([high, low], axis=1),
            jnp.concatenate([high, jnp.zeros_like(low)], axis=1),
        ],
        axis=0,
    )
    both = jnp.dot(sides, right, preferred_element_type=jnp.float32)
    return both[:, :size] + both[:, size:]


def own_state_kernel(place, ends, mixed_b, out):
    out[...] = state_of(ends[...], mixed_b[...])


def sent_state_kernel(headdim, place, ends, mixed_b, logs, out):
    state = state_of(ends[...], mixed_b[...])
    rows, size = state.shape
    heads = rows // headdim
    codes, scale = code_states(state.reshape(heads, headdim, size))
    out[0:rows, :] = codes.reshape(rows, size)
    out[rows : rows + heads, :] = scale
    high, low = code_logs(logs[...])
    out[rows + heads : rows + 2 * heads, :] = high
    out[rows + 2 * heads : rows + 3 * heads, :] = low


def kept_state_kernel(kepts, mixed_b, out):
    out[...] = state_of(kepts[...], mixed_b[...])


def group_kernel(headdim, place, own, own_logs, got1, got2, got3, prefix, decay, sent, held, logs):
    rows, size = own.shape
    heads = rows // headdim
    first = place[0]
    held[first] = own[...]
    logs[first] = own_logs[...]
    for step, got in ((1, got1), (2, got2), (3, got3)):
        shard = first ^ step
        state = read_states(
            got[0:rows, :].reshape(heads, headdim, size), got[rows : rows + heads, :]
        )
        held[shard] = state.reshape(rows, size)
        logs[shard] = read_logs(
            got[rows + heads : rows + 2 * heads, :], got[rows + 2 * heads : rows + 3 * heads, :]
        )
    carried = jnp.zeros((heads, headdim, size), jnp.float32)
    passed = jnp.zeros((heads, size), jnp.float32)
    for shard in range(GROUP):
        prefix[shard] = carried.reshape(rows, size)
        decay[shard] = jnp.exp(passed)
        step_log = logs[shard]
        state = held[shard].reshape(heads, headdim, size)
        carried = jnp.exp(step_log)[:, None, :] * carried + state
        passed = passed + step_log
    codes, scale = code_states(carried)
    high, low = code_logs(passed)
    rest = jnp.zeros((heads, ROWS - 3, size), jnp.int32)
    notes = jnp.concatenate(
        [a.astype(jnp.int32)[:, None, :] for a in (scale, high, low)] + [rest], axis=1
    )
    sent[:, 0:headdim, :] = codes
    sent[:, headdim : headdim + ROWS, :] = notes.astype(jnp.int16)


def scan_kernel(headdim, got, sent):
    groups, size = got.shape[0], got.shape[2]
    carried = jnp.zeros((1, headdim, size), jnp.float32)
    for group in range(groups):
        codes, scale = code_states(carried)
        sent[group, 0:headdim, :] = codes[0]
        sent[group, headdim : headdim + ROWS, :] = jnp.broadcast_to(
            scale.astype(jnp.int32), (ROWS, size)
        ).astype(jnp.int16)
        notes = got[group, headdim : headdim + ROWS, :].astype(jnp.int32)
        state = read_states(got[group, 0:headdim, :][None], notes[0:1])
        log = read_logs(notes[1:2], notes[2:3])
        carried = jnp.exp(log)[:, None, :] * carried + state


def group_incoming(headdim, got, prefix, decay):
    size = got.shape[2]
    notes = got[:, headdim : headdim + ROWS, :].astype(jnp.int32)
    state = read_states(got[:, 0:headdim, :], notes[:, 0, :])
    local = prefix[0].reshape(-1, headdim, size)
    return decay[0][:, None, :] * state + local


def own_incoming_kernel(headdim, place, got, prefix, decay, out):
    out[...] = group_incoming(headdim, got, prefix, decay).reshape(out.shape)


def sent_incoming_kernel(headdim, place, got, prefix, decay, out):
    incoming = group_incoming(headdim, got, prefix, decay)
    heads, headdim, size = incoming.shape
    codes, scale = code_states(incoming)
    out[0 : heads * headdim, :] = codes.reshape(heads * headdim, size)
    out[heads * headdim :, :] = scale


def final_kernel(headdim, place, own, got1, got2, got3, kept, part, out):
    rows, size = own.shape
    heads = rows // headdim

    def place_slice(step, incoming):
        slot = place[0] ^ step
        lines = pl.ds(pl.multiple_of(slot * rows, rows), rows)
        heads_here = pl.ds(pl.multiple_of(slot * heads, heads), heads)
        scaled = kept[heads_here, :][:, None, :] * incoming
        out[lines, :] = scaled.reshape(rows, size) + part[lines, :]

    place_slice(0, own[...].reshape(heads, headdim, size))
    for step, got in ((1, got1), (2, got2), (3, got3)):
        place_slice(
            step,
            read_states(got[0:rows, :].reshape(heads, headdim, size), got[rows : rows + heads, :]),
        )


def whole(shape):
    return pl.BlockSpec(shape, lambda *_: (0,) * len(shape))


def gridded(kernel, grid, in_specs, out_specs, out_shape, scratch=()):
    return call(
        kernel,
        grid_spec=pltpu.PrefetchScalarGridSpec(
            num_scalar_prefetch=1,
            grid=grid,
            in_specs=in_specs,
            out_specs=out_specs,
            scratch_shapes=scratch,
        ),
        out_shape=out_shape,
    )


def on_device(hidden, inputs, w_b, conv_x, conv_b, log_decay, accepted):
    tokens = hidden[0]
    values = inputs[0]
    length, width = tokens.shape
    channels = values.shape[1]
    margin = conv_x.shape[0] - 1
    head_count = log_decay.shape[2]
    headdim = channels // head_count
    size = w_b.shape[1]
    depth = w_b.shape[0]
    heads = head_count // GROUP
    rows = heads * headdim
    f32, bf16, i16 = jnp.float32, jnp.bfloat16, jnp.int16

    shards = lax.axis_size("seq")
    parts = lax.axis_size("fsdp")
    shard = lax.axis_index("seq")
    place = jnp.stack([shard % GROUP, lax.axis_index("fsdp")]).astype(jnp.int32)

    ends = jnp.concatenate([tokens[length - margin :], values[length - margin :]], 1)
    before = lax.ppermute(ends, "seq", [(i, i + 1) for i in range(shards - 1)])
    tail = jnp.pad(before, ((ROWS - margin, 0), (0, 0)))
    w_own = [w_b] + [
        lax.ppermute(w_b, "fsdp", [(i, i ^ (2 * step)) for i in range(parts)])
        for step in (1, 2, 3)
    ]
    w_other = lax.ppermute(jnp.stack(w_own), "fsdp", [(i, i ^ 1) for i in range(parts)])

    prefix = jnp.concatenate(
        [jnp.zeros((1, head_count), f32), jnp.cumsum(log_decay[0], axis=0)], 0
    )
    kept = accepted[0, 0]
    end_logs = prefix[length]
    chosen = (jnp.arange(length + 1) == kept).astype(f32)
    kept_log = jnp.sum(chosen[:, None] * prefix, axis=0)
    after = prefix[1:].T
    inside = (jnp.arange(length) < kept)[None, :]
    weight_end = jnp.exp(end_logs[:, None] - after)
    weight_kept = jnp.where(
        inside, jnp.exp(jnp.where(inside, kept_log[:, None] - after, 0.0)), 0.0
    )
    wide_logs = jnp.broadcast_to(end_logs[:, None], (head_count, size))
    wide_kept = jnp.broadcast_to(jnp.exp(kept_log)[:, None], (head_count, size))

    sides = jax.ShapeDtypeStruct((channels, 2 * length), bf16)
    ends_x, kepts_x = call(
        mixed_x_kernel,
        grid=(GROUP,),
        in_specs=[
            pl.BlockSpec((length, rows), lambda i: (0, i)),
            pl.BlockSpec((ROWS, rows), lambda i: (0, i)),
            pl.BlockSpec((margin + 1, rows), lambda i: (0, i)),
            pl.BlockSpec((heads, length), lambda i: (i, 0)),
            pl.BlockSpec((heads, length), lambda i: (i, 0)),
        ],
        out_specs=[pl.BlockSpec((rows, 2 * length), lambda i: (i, 0))] * 2,
        out_shape=[sides, sides],
        scratch_shapes=[pltpu.VMEM((ROWS + length, rows), f32)],
    )(values, tail[:, width:], conv_x, weight_end, weight_kept)

    begun = gridded(
        partial_kernel,
        (1,),
        [whole((length, width)), whole((ROWS, width))] + [whole((depth, size))] * GROUP,
        whole((ROWS + length, size)),
        jax.ShapeDtypeStruct((ROWS + length, size), f32),
    )(place, tokens, tail[:, :width], *w_own)
    mixed_b = gridded(
        mixed_b_kernel,
        (1,),
        [
            whole((length, width)),
            whole((ROWS, width)),
            whole((GROUP, depth, size)),
            whole((margin + 1, size)),
            whole((ROWS + length, size)),
        ],
        whole((length, size)),
        jax.ShapeDtypeStruct((length, size), f32),
        [pltpu.VMEM((ROWS + length, size), f32)],
    )(place, tokens, tail[:, :width], w_other, conv_b, begun)

    def slice_of(step):
        return lambda i, place: (place[0] ^ step, 0)

    pairs = [[(i, i ^ step) for i in range(shards)] for step in range(GROUP)]
    got = []
    for step in (2, 3, 1):
        sent = gridded(
            functools.partial(sent_state_kernel, headdim),
            (1,),
            [
                pl.BlockSpec((rows, 2 * length), slice_of(step)),
                whole((length, size)),
                pl.BlockSpec((heads, size), slice_of(step)),
            ],
            whole((rows + 3 * heads, size)),
            jax.ShapeDtypeStruct((rows + 3 * heads, size), i16),
        )(place, ends_x, mixed_b, wide_logs)
        got.append(lax.ppermute(sent, "seq", pairs[step]))
    got = [got[2], got[0], got[1]]
    own = gridded(
        own_state_kernel,
        (1,),
        [pl.BlockSpec((rows, 2 * length), slice_of(0)), whole((length, size))],
        whole((rows, size)),
        jax.ShapeDtypeStruct((rows, size), f32),
    )(place, ends_x, mixed_b)
    part = call(
        kept_state_kernel,
        grid=(GROUP,),
        in_specs=[pl.BlockSpec((rows, 2 * length), lambda i: (i, 0)), whole((length, size))],
        out_specs=pl.BlockSpec((rows, size), lambda i: (i, 0)),
        out_shape=jax.ShapeDtypeStruct((channels, size), f32),
    )(kepts_x, mixed_b)

    groups = shards // GROUP
    message = (heads, headdim + ROWS, size)
    prefix_states, prefix_decay, sent = gridded(
        functools.partial(group_kernel, headdim),
        (1,),
        [whole((rows, size)), pl.BlockSpec((heads, size), slice_of(0))]
        + [whole((rows + 3 * heads, size))] * 3,
        [whole((GROUP, rows, size)), whole((GROUP, heads, size)), whole(message)],
        [
            jax.ShapeDtypeStruct((GROUP, rows, size), f32),
            jax.ShapeDtypeStruct((GROUP, heads, size), f32),
            jax.ShapeDtypeStruct(message, i16),
        ],
        [pltpu.VMEM((GROUP, rows, size), f32), pltpu.VMEM((GROUP, heads, size), f32)],
    )(place, own, wide_logs, *got)
    members = [[g * GROUP + b for g in range(groups)] for b in range(GROUP)]
    totals = lax.all_to_all(sent, "seq", 0, 0, axis_index_groups=members)
    scanned = call(
        functools.partial(scan_kernel, headdim),
        out_shape=jax.ShapeDtypeStruct(message, i16),
    )(totals)
    carried = lax.all_to_all(scanned, "seq", 0, 0, axis_index_groups=members)

    def incoming(kernel, step, out_rows, kind):
        return gridded(
            functools.partial(kernel, headdim),
            (1,),
            [
                whole(message),
                pl.BlockSpec((1, rows, size), lambda i, place: (place[0] ^ step, 0, 0)),
                pl.BlockSpec((1, heads, size), lambda i, place: (place[0] ^ step, 0, 0)),
            ],
            whole((out_rows, size)),
            jax.ShapeDtypeStruct((out_rows, size), kind),
        )(place, carried, prefix_states, prefix_decay)

    back = []
    for step in (2, 3, 1):
        sent = incoming(sent_incoming_kernel, step, rows + heads, i16)
        back.append(lax.ppermute(sent, "seq", pairs[step]))
    back = [back[2], back[0], back[1]]
    own = incoming(own_incoming_kernel, 0, rows, f32)
    final = gridded(
        functools.partial(final_kernel, headdim),
        (1,),
        [whole((rows, size))]
        + [whole((rows + heads, size))] * 3
        + [whole((head_count, size)), whole((channels, size))],
        whole((channels, size)),
        jax.ShapeDtypeStruct((channels, size), f32),
    )(place, own, *back, wide_kept, part)
    return final.reshape(1, 1, head_count, headdim, size)


def solution(mesh):
    placed = (
        P("fsdp", "seq", None),
        P("fsdp", "seq", None),
        P("fsdp", None),
        P(),
        P(),
        P("fsdp", "seq", None),
        P("fsdp", "seq"),
    )
    return jax.shard_map(
        on_device,
        mesh=mesh,
        in_specs=placed,
        out_specs=P("fsdp", "seq", None, None, None),
        check_vma=False,
    )
```

time: 665 us -> 122 us (0.18)
  the two profiles are of different devices: /device:TPU:504 before, /device:TPU:6 now
where the time goes in v1:
time: 122 us
  blocking collectives  53.4 us (44%)
  starting transfers between devices  37.1 us (30%)
  waiting for transfers between devices  13 us (11%)
  Pallas kernels  12.9 us (11%)
  local copies, waits for them, and re-layouts  2.84 us (2%)
  other arithmetic  1.47 us (1%)
    all_to_all x1, blocking collectives, on_device(): totals = lax.all_to_all(sent, 'seq', 0, 0, axis_index_groups=members)  32.5 us
    all_to_all x1, blocking collectives, on_device(): carried = lax.all_to_all(scanned, 'seq', 0, 0, axis_index_groups=members)  20.9 us
    ppermute x3, starting transfers between devices, on_device(): lax.ppermute(w_b, 'fsdp', [(i, i ^ 2 * step) for i in range(parts)])  13.2 us
    ppermute x3, starting transfers between devices, on_device(): got.append(lax.ppermute(sent, 'seq', pairs[step]))  10.6 us
    ppermute x3, starting transfers between devices, on_device(): back.append(lax.ppermute(sent, 'seq', pairs[step]))  10.1 us
    ppermute x3, waiting for transfers between devices, on_device(): got.append(lax.ppermute(sent, 'seq', pairs[step]))  7.59 us
    ppermute x3, waiting for transfers between devices, on_device(): back.append(lax.ppermute(sent, 'seq', pairs[step]))  3.91 us
    pallas_call x4, Pallas kernels, incoming(): gridded(functools.partial(kernel, headdim), (1,), [whole(message), pl.Blo...  2.67 us
  transfers between devices with their start and end apart: 11, of which 5 were waited for; matrix products, arithmetic and copies ran while one was open for 3% of the time, Pallas kernels for 5%

profile of v1, /device:TPU:6, one launch (start us, length us, event | category | flops | bytes accessed | tf_op | source)
XLA Modules:
  0.0 121.8 jit_solution(873893398821300069)
XLA Ops:
  0.0 2.9 %collective-permute-start.1 = (bf16[640,128]{1,0:T(8,128)(2,1)}, bf16[640,128]{1,0:T(8,128)(2,1)S(1)}, u32[]{:S(2)}, u32[]{:S(2)}) collective-permute-start(bf16[640,128]{1,0:T(8,128)(2,1)} %w0.1), channel_id=1, source_target_pairs={{0,2},{1,3},{2,0},{3,1},{4,6},{5,7},{6,4},{7,5},{8,10},{9,11},{10,... | collective-permute-start | bytes 491528 | tf_op jit(solution)/shard_map/ppermute | solution.py:265
  2.9 8.4 %collective-permute-start.2 = (bf16[640,128]{1,0:T(8,128)(2,1)}, bf16[640,128]{1,0:T(8,128)(2,1)S(1)}, u32[]{:S(2)}, u32[]{:S(2)}) collective-permute-start(bf16[640,128]{1,0:T(8,128)(2,1)} %w0.1), channel_id=1, source_target_pairs={{0,4},{1,5},{2,6},{3,7},{4,0},{5,1},{6,2},{7,3},{8,12},{9,13},{10,... | collective-permute-start | bytes 491528 | tf_op jit(solution)/shard_map/ppermute | solution.py:265
  11.3 1.9 %collective-permute-start.3 = (bf16[640,128]{1,0:T(8,128)(2,1)}, bf16[640,128]{1,0:T(8,128)(2,1)S(1)}, u32[]{:S(2)}, u32[]{:S(2)}) collective-permute-start(bf16[640,128]{1,0:T(8,128)(2,1)} %w0.1), channel_id=1, source_target_pairs={{0,6},{1,7},{2,4},{3,5},{4,2},{5,3},{6,0},{7,1},{8,14},{9,15},{10,... | collective-permute-start | bytes 491528 | tf_op jit(solution)/shard_map/ppermute | solution.py:265
  13.2 0.9 slice_bitcast_fusion
  14.1 0.8 slice_bitcast_fusion.1
  14.9 1.3 %collective-permute-start = (bf16[3,7168]{1,0:T(4,128)(2,1)S(1)}, bf16[3,7168]{1,0:T(4,128)(2,1)S(1)}, u32[]{:S(2)}, u32[]{:S(2)}) collective-permute-start(bf16[3,7168]{1,0:T(4,128)(2,1)S(1)} %pad_maximum_fusion.1), channel_id=1, source_target_pairs={{0,8},{8,16},{16,24},{24,32},{32,40},{40,48},{48,56},{56,64},{64,7... | collective-permute-start | bytes 129032 | tf_op jit(solution)/shard_map/ppermute | solution.py:262
  16.2 0.8 copy.8
  18.4 1.5 %collective-permute-done.3.w3 = bf16[640,128]{1,0:T(8,128)(2,1)S(1)} collective-permute-done((bf16[640,128]{1,0:T(8,128)(2,1)}, bf16[640,128]{1,0:T(8,128)(2,1)S(1)}, u32[]{:S(2)}, u32[]{:S(2)}) %collective-permute-start.3) | collective-permute-done | bytes 163872 | tf_op jit(solution)/shard_map/ppermute | solution.py:265
  19.9 1.0 pad_maximum_fusion
  20.9 1.9 %collective-permute-start.4 = (bf16[4,640,128]{2,1,0:T(8,128)(2,1)S(1)}, bf16[4,640,128]{2,1,0:T(8,128)(2,1)S(1)}, u32[]{:S(2)}, u32[]{:S(2)}) collective-permute-start(bf16[4,640,128]{2,1,0:T(8,128)(2,1)S(1)} %pad_maximum_fusion), channel_id=1, source_target_pairs={{0,1},{1,0},{2,3},{3,2},{4,5},{5,4},{6,7},{7,6},{8,9},{9,8},{10,11... | collective-permute-start | bytes 1966088 | tf_op jit(solution)/shard_map/ppermute | solution.py:268
  22.9 1.2 shard_map.73
  24.2 1.0 shard_map.74.begun
  25.2 1.0 shard_map.75.mixed_b
  26.3 0.8 shard_map.79
  27.1 0.8 shard_map.78
  27.9 0.8 shard_map.77
  28.8 6.2 %collective-permute-start.7 = (s16[560,128]{1,0:T(8,128)(2,1)S(1)}, s16[560,128]{1,0:T(8,128)(2,1)S(1)}, u32[]{:S(2)}, u32[]{:S(2)}) collective-permute-start(s16[560,128]{1,0:T(8,128)(2,1)S(1)} %shard_map.79), channel_id=1, source_target_pairs={{0,24},{8,16},{16,8},{24,0},{32,56},{40,48},{48,40},{56,32},{64,88... | collective-permute-start | bytes 430088 | tf_op jit(solution)/shard_map/ppermute | solution.py:341
  35.0 1.9 %collective-permute-start.6 = (s16[560,128]{1,0:T(8,128)(2,1)S(1)}, s16[560,128]{1,0:T(8,128)(2,1)S(1)}, u32[]{:S(2)}, u32[]{:S(2)}) collective-permute-start(s16[560,128]{1,0:T(8,128)(2,1)S(1)} %shard_map.78), channel_id=1, source_target_pairs={{0,16},{8,24},{16,0},{24,8},{32,48},{40,56},{48,32},{56,40},{64,80... | collective-permute-start | bytes 430088 | tf_op jit(solution)/shard_map/ppermute | solution.py:341
  36.9 2.5 %collective-permute-start.5 = (s16[560,128]{1,0:T(8,128)(2,1)S(1)}, s16[560,128]{1,0:T(8,128)(2,1)S(1)}, u32[]{:S(2)}, u32[]{:S(2)}) collective-permute-start(s16[560,128]{1,0:T(8,128)(2,1)S(1)} %shard_map.77), channel_id=1, source_target_pairs={{0,8},{8,0},{16,24},{24,16},{32,40},{40,32},{48,56},{56,48},{64,72... | collective-permute-start | bytes 430088 | tf_op jit(solution)/shard_map/ppermute | solution.py:341
  39.4 0.8 shard_map.76.own
  40.2 6.0 %collective-permute-done.6.got2 = s16[560,128]{1,0:T(8,128)(2,1)S(1)} collective-permute-done((s16[560,128]{1,0:T(8,128)(2,1)S(1)}, s16[560,128]{1,0:T(8,128)(2,1)S(1)}, u32[]{:S(2)}, u32[]{:S(2)}) %collective-permute-start.6) | collective-permute-done | bytes 143392 | tf_op jit(solution)/shard_map/ppermute | solution.py:341
  46.1 1.6 %collective-permute-done.5.got1 = s16[560,128]{1,0:T(8,128)(2,1)S(1)} collective-permute-done((s16[560,128]{1,0:T(8,128)(2,1)S(1)}, s16[560,128]{1,0:T(8,128)(2,1)S(1)}, u32[]{:S(2)}, u32[]{:S(2)}) %collective-permute-start.5) | collective-permute-done | bytes 143392 | tf_op jit(solution)/shard_map/ppermute | solution.py:341
  47.7 0.9 shard_map.80
  48.7 32.5 %all_to_all.10.got = s16[16,48,128]{2,1,0:T(8,128)(2,1)S(1)} all-to-all(s16[16,48,128]{2,1,0:T(8,128)(2,1)S(1)} %get-tuple-element.11), channel_id=1, replica_groups={{0,32,64,96,128,160,192,224,256,288,320,352,384,416,448,480},{8,40,72,1..., dimensions={0} | all-to-all | bytes 393216 | tf_op jit(solution)/shard_map/all_to_all | solution.py:374
  81.3 20.9 %all_to_all.11.got = s16[16,48,128]{2,1,0:T(8,128)(2,1)S(1)} all-to-all(s16[16,48,128]{2,1,0:T(8,128)(2,1)S(1)} %shard_map.81), channel_id=1, replica_groups={{0,32,64,96,128,160,192,224,256,288,320,352,384,416,448,480},{8,40,72,1..., dimensions={0} | all-to-all | bytes 393216 | tf_op jit(solution)/shard_map/all_to_all | solution.py:379
  102.9 3.9 %collective-permute-start.10 = (s16[528,128]{1,0:T(8,128)(2,1)S(1)}, s16[528,128]{1,0:T(8,128)(2,1)S(1)}, u32[]{:S(2)}, u32[]{:S(2)}) collective-permute-start(s16[528,128]{1,0:T(8,128)(2,1)S(1)} %shard_map.85), channel_id=1, source_target_pairs={{0,24},{8,16},{16,8},{24,0},{32,56},{40,48},{48,40},{56,32},{64,88... | collective-permute-start | bytes 405512 | tf_op jit(solution)/shard_map/ppermute | solution.py:397
  107.5 3.8 %collective-permute-start.9 = (s16[528,128]{1,0:T(8,128)(2,1)S(1)}, s16[528,128]{1,0:T(8,128)(2,1)S(1)}, u32[]{:S(2)}, u32[]{:S(2)}) collective-permute-start(s16[528,128]{1,0:T(8,128)(2,1)S(1)} %shard_map.84), channel_id=1, source_target_pairs={{0,16},{8,24},{16,0},{24,8},{32,48},{40,56},{48,32},{56,40},{64,80... | collective-permute-start | bytes 405512 | tf_op jit(solution)/shard_map/ppermute | solution.py:397
  112.0 2.4 %collective-permute-start.8 = (s16[528,128]{1,0:T(8,128)(2,1)S(1)}, s16[528,128]{1,0:T(8,128)(2,1)S(1)}, u32[]{:S(2)}, u32[]{:S(2)}) collective-permute-start(s16[528,128]{1,0:T(8,128)(2,1)S(1)} %shard_map.83), channel_id=1, source_target_pairs={{0,8},{8,0},{16,24},{24,16},{32,40},{40,32},{48,56},{56,48},{64,72... | collective-permute-start | bytes 405512 | tf_op jit(solution)/shard_map/ppermute | solution.py:397
  114.4 0.9 shard_map.86.part
  116.0 2.6 %collective-permute-done.9.got2 = s16[528,128]{1,0:T(8,128)(2,1)S(1)} collective-permute-done((s16[528,128]{1,0:T(8,128)(2,1)S(1)}, s16[528,128]{1,0:T(8,128)(2,1)S(1)}, u32[]{:S(2)}, u32[]{:S(2)}) %collective-permute-start.9) | collective-permute-done | bytes 135200 | tf_op jit(solution)/shard_map/ppermute | solution.py:397
  118.6 1.3 %collective-permute-done.8.got1 = s16[528,128]{1,0:T(8,128)(2,1)S(1)} collective-permute-done((s16[528,128]{1,0:T(8,128)(2,1)S(1)}, s16[528,128]{1,0:T(8,128)(2,1)S(1)}, u32[]{:S(2)}, u32[]{:S(2)}) %collective-permute-start.8) | collective-permute-done | bytes 135200 | tf_op jit(solution)/shard_map/ppermute | solution.py:397
  120.0 1.8 %shard_map.87 = f32[2048,128]{1,0:T(8,128)} custom-call(s32[2]{0:T(128)S(1)} %pad_add_fusion.place, f32[512,128]{1,0:T(8,128)S(1)} %shard_map.82.own, s16[528,128]{1,0:T(8,128)(2,1)S(1)} %collective-permute-done.8.got1, s16[528,128]{1,0:T(8,128)(2,1)S(1)} %collective-permute-done.9.got2, s16[528,128]{1,0:T(8,128)(2,1)S(1)} %collective-permute-done.10.got3, ...), custom_call_target="tpu_custom_call" | custom-call | tf_op jit(solution)/shard_map/pallas_call | solution.py:400
  (35 shorter events, 3.6 us)
Async XLA Ops:
  0.0 22.9 %copy-start.2 = (bf16[1,128,2048]{2,1,0:T(8,128)(2,1)S(1)}, bf16[1,128,2048]{2,1,0:T(8,128)(2,1)}, u32[]{:S(2)}) copy-start(bf16[1,128,2048]{2,1,0:T(8,128)(2,1)} %param.8) | copy-start | bytes 1572868
  0.0 22.9 %copy-start.3 = (f32[4,2048]{1,0:T(4,128)S(1)}, f32[4,2048]{1,0:T(4,128)}, u32[]{:S(2)}) copy-start(f32[4,2048]{1,0:T(4,128)} %taps.2) | copy-start | bytes 98308
  0.0 18.4 %collective-permute-start.1 = (bf16[640,128]{1,0:T(8,128)(2,1)}, bf16[640,128]{1,0:T(8,128)(2,1)S(1)}, u32[]{:S(2)}, u32[]{:S(2)}) collective-permute-start(bf16[640,128]{1,0:T(8,128)(2,1)} %w0.1), channel_id=1, source_target_pairs={{0,2},{1,3},{2,0},{3,1},{4,6},{5,7},{6,4},{7,5},{8,10},{9,11},{10,... | collective-permute-start | bytes 491528 | tf_op jit(solution)/shard_map/ppermute | solution.py:265
  2.9 15.6 %collective-permute-start.2 = (bf16[640,128]{1,0:T(8,128)(2,1)}, bf16[640,128]{1,0:T(8,128)(2,1)S(1)}, u32[]{:S(2)}, u32[]{:S(2)}) collective-permute-start(bf16[640,128]{1,0:T(8,128)(2,1)} %w0.1), channel_id=1, source_target_pairs={{0,4},{1,5},{2,6},{3,7},{4,0},{5,1},{6,2},{7,3},{8,12},{9,13},{10,... | collective-permute-start | bytes 491528 | tf_op jit(solution)/shard_map/ppermute | solution.py:265
  11.3 8.6 %collective-permute-start.3 = (bf16[640,128]{1,0:T(8,128)(2,1)}, bf16[640,128]{1,0:T(8,128)(2,1)S(1)}, u32[]{:S(2)}, u32[]{:S(2)}) collective-permute-start(bf16[640,128]{1,0:T(8,128)(2,1)} %w0.1), channel_id=1, source_target_pairs={{0,6},{1,7},{2,4},{3,5},{4,2},{5,3},{6,0},{7,1},{8,14},{9,15},{10,... | collective-permute-start | bytes 491528 | tf_op jit(solution)/shard_map/ppermute | solution.py:265
  14.9 7.9 %collective-permute-start = (bf16[3,7168]{1,0:T(4,128)(2,1)S(1)}, bf16[3,7168]{1,0:T(4,128)(2,1)S(1)}, u32[]{:S(2)}, u32[]{:S(2)}) collective-permute-start(bf16[3,7168]{1,0:T(4,128)(2,1)S(1)} %pad_maximum_fusion.1), channel_id=1, source_target_pairs={{0,8},{8,16},{16,24},{24,32},{32,40},{40,48},{48,56},{56,64},{64,7... | collective-permute-start | bytes 129032 | tf_op jit(solution)/shard_map/ppermute | solution.py:262
  17.3 6.8 %copy-start = (bf16[1,128,5120]{2,1,0:T(8,128)(2,1)S(1)}, bf16[1,128,5120]{2,1,0:T(8,128)(2,1)}, u32[]{:S(2)}) copy-start(bf16[1,128,5120]{2,1,0:T(8,128)(2,1)} %param.7) | copy-start | bytes 3932164
  17.4 6.8 %copy-start.1 = (bf16[640,128]{1,0:T(8,128)(2,1)S(1)}, bf16[640,128]{1,0:T(8,128)(2,1)}, u32[]{:S(2)}) copy-start(bf16[640,128]{1,0:T(8,128)(2,1)} %w0.1) | copy-start | bytes 491524
  20.9 4.3 %collective-permute-start.4 = (bf16[4,640,128]{2,1,0:T(8,128)(2,1)S(1)}, bf16[4,640,128]{2,1,0:T(8,128)(2,1)S(1)}, u32[]{:S(2)}, u32[]{:S(2)}) collective-permute-start(bf16[4,640,128]{2,1,0:T(8,128)(2,1)S(1)} %pad_maximum_fusion), channel_id=1, source_target_pairs={{0,1},{1,0},{2,3},{3,2},{4,5},{5,4},{6,7},{7,6},{8,9},{9,8},{10,11... | collective-permute-start | bytes 1966088 | tf_op jit(solution)/shard_map/ppermute | solution.py:268
  24.1 1.1 copy-start.4
  28.8 11.4 %collective-permute-start.7 = (s16[560,128]{1,0:T(8,128)(2,1)S(1)}, s16[560,128]{1,0:T(8,128)(2,1)S(1)}, u32[]{:S(2)}, u32[]{:S(2)}) collective-permute-start(s16[560,128]{1,0:T(8,128)(2,1)S(1)} %shard_map.79), channel_id=1, source_target_pairs={{0,24},{8,16},{16,8},{24,0},{32,56},{40,48},{48,40},{56,32},{64,88... | collective-permute-start | bytes 430088 | tf_op jit(solution)/shard_map/ppermute | solution.py:341
  35.0 11.2 %collective-permute-start.6 = (s16[560,128]{1,0:T(8,128)(2,1)S(1)}, s16[560,128]{1,0:T(8,128)(2,1)S(1)}, u32[]{:S(2)}, u32[]{:S(2)}) collective-permute-start(s16[560,128]{1,0:T(8,128)(2,1)S(1)} %shard_map.78), channel_id=1, source_target_pairs={{0,16},{8,24},{16,0},{24,8},{32,48},{40,56},{48,32},{56,40},{64,80... | collective-permute-start | bytes 430088 | tf_op jit(solution)/shard_map/ppermute | solution.py:341
  36.9 10.9 %collective-permute-start.5 = (s16[560,128]{1,0:T(8,128)(2,1)S(1)}, s16[560,128]{1,0:T(8,128)(2,1)S(1)}, u32[]{:S(2)}, u32[]{:S(2)}) collective-permute-start(s16[560,128]{1,0:T(8,128)(2,1)S(1)} %shard_map.77), channel_id=1, source_target_pairs={{0,8},{8,0},{16,24},{24,16},{32,40},{40,32},{48,56},{56,48},{64,72... | collective-permute-start | bytes 430088 | tf_op jit(solution)/shard_map/ppermute | solution.py:341
  102.9 13.1 %collective-permute-start.10 = (s16[528,128]{1,0:T(8,128)(2,1)S(1)}, s16[528,128]{1,0:T(8,128)(2,1)S(1)}, u32[]{:S(2)}, u32[]{:S(2)}) collective-permute-start(s16[528,128]{1,0:T(8,128)(2,1)S(1)} %shard_map.85), channel_id=1, source_target_pairs={{0,24},{8,16},{16,8},{24,0},{32,56},{40,48},{48,40},{56,32},{64,88... | collective-permute-start | bytes 405512 | tf_op jit(solution)/shard_map/ppermute | solution.py:397
  107.5 11.1 %collective-permute-start.9 = (s16[528,128]{1,0:T(8,128)(2,1)S(1)}, s16[528,128]{1,0:T(8,128)(2,1)S(1)}, u32[]{:S(2)}, u32[]{:S(2)}) collective-permute-start(s16[528,128]{1,0:T(8,128)(2,1)S(1)} %shard_map.84), channel_id=1, source_target_pairs={{0,16},{8,24},{16,0},{24,8},{32,48},{40,56},{48,32},{56,40},{64,80... | collective-permute-start | bytes 405512 | tf_op jit(solution)/shard_map/ppermute | solution.py:397
  112.0 7.9 %collective-permute-start.8 = (s16[528,128]{1,0:T(8,128)(2,1)S(1)}, s16[528,128]{1,0:T(8,128)(2,1)S(1)}, u32[]{:S(2)}, u32[]{:S(2)}) collective-permute-start(s16[528,128]{1,0:T(8,128)(2,1)S(1)} %shard_map.83), channel_id=1, source_target_pairs={{0,8},{8,0},{16,24},{24,16},{32,40},{40,32},{48,56},{56,48},{64,72... | collective-permute-start | bytes 405512 | tf_op jit(solution)/shard_map/ppermute | solution.py:397

commit v2 on v0

v2 whole, which is shorter than its diff:
```python
import functools

import jax
import jax.numpy as jnp
from jax import lax
from jax.experimental import pallas as pl
from jax.experimental.pallas import tpu as pltpu
from jax.sharding import PartitionSpec as P

ROWS = 16
GROUP = 4
TOP = 32760.0
FINE = 128.0
LOG_STEP = float(2**19)
VMEM = 12 * 1024 * 1024


def call(kernel, *args, out, scratch=(), far=()):
    places = [
        pltpu.SMEM if a.shape == (1,) else pltpu.HBM if i in far else pltpu.VMEM
        for i, a in enumerate(args)
    ]
    return pl.pallas_call(
        kernel,
        in_specs=[pl.BlockSpec(memory_space=place) for place in places],
        out_specs=jax.tree.map(lambda _: pl.BlockSpec(memory_space=pltpu.VMEM), out),
        out_shape=out,
        scratch_shapes=scratch,
        compiler_params=pltpu.CompilerParams(vmem_limit_bytes=VMEM),
    )(*args)


def scale_codes(top):
    return jnp.ceil(jnp.log2(jnp.maximum(top, 1e-33)) * FINE)


def up(scale):
    return TOP * jnp.exp2(scale * (-1.0 / FINE))


def down(scale):
    return jnp.exp2(scale * (1.0 / FINE)) * (1.0 / TOP)


def pack(high, low):
    return lax.shift_left(high, 16) | (low & 0xFFFF)


def high_of(words):
    return lax.shift_right_arithmetic(words, 16)


def low_of(words):
    return lax.shift_right_arithmetic(lax.shift_left(words, 16), 16)


def words_of(scaled):
    codes = jnp.round(scaled).astype(jnp.int32)
    half = codes.shape[-2] // 2
    return pack(codes[..., :half, :], codes[..., half:, :])


def codes_of(words):
    return jnp.concatenate([high_of(words), low_of(words)], axis=-2).astype(jnp.float32)


def code_logs(logs):
    whole = jnp.round(logs * -LOG_STEP).astype(jnp.int32)
    lane = lax.broadcasted_iota(jnp.int32, logs.shape, 1)
    high = lax.shift_right_logical(whole, 15)
    return jnp.where(lane < logs.shape[1] // 2, high, whole & 0x7FFF)


def read_logs(notes):
    lane = lax.broadcasted_iota(jnp.int32, notes.shape, 1)
    parts = (notes & 0xFFFF).astype(jnp.float32)
    high = jnp.sum(jnp.where(lane == 0, parts, 0.0), axis=1, keepdims=True)
    low = jnp.sum(jnp.where(lane == notes.shape[1] - 1, parts, 0.0), axis=1, keepdims=True)
    return (high * 32768.0 + low) * (-1.0 / LOG_STEP)


def moved(pairs, arrived):
    moves = [
        pltpu.make_async_copy(source, target, arrived.at[i])
        for i, (source, target) in enumerate(pairs)
    ]
    for move in moves:
        move.start()
    for move in moves:
        move.wait()


def copies_kernel(w, out, held, arrived):
    moved([(w, held)], arrived)
    moved([(held, out.at[copy]) for copy in range(out.shape[0])], arrived)


def copies(w, count):
    return pl.pallas_call(
        copies_kernel,
        in_specs=[pl.BlockSpec(memory_space=pltpu.HBM)],
        out_specs=pl.BlockSpec(memory_space=pltpu.HBM),
        out_shape=jax.ShapeDtypeStruct((count, *w.shape), w.dtype),
        scratch_shapes=[pltpu.VMEM(w.shape, w.dtype), pltpu.SemaphoreType.DMA((count,))],
        compiler_params=pltpu.CompilerParams(vmem_limit_bytes=VMEM),
    )(w)


def edge_kernel(tokens, values, out, last_tokens, last_values, arrived):
    lines = pl.ds(tokens.shape[0] - ROWS, ROWS)
    moved([(tokens.at[lines, :], last_tokens), (values.at[lines, :], last_values)], arrived)
    margin, width = out.shape[0], tokens.shape[1]
    out[:, :width] = last_tokens[...].astype(jnp.float32)[ROWS - margin :, :].astype(out.dtype)
    out[:, width:] = last_values[...].astype(jnp.float32)[ROWS - margin :, :].astype(out.dtype)


def columns_of(chip, core, depth):
    return pl.ds(pl.multiple_of((2 * chip + core) * depth, 128), depth)


def project(core, hidden, tail, w, main, edge):
    depth = w.shape[1]
    for chip in range(w.shape[0]):
        some = hidden[:, chip * depth : (chip + 1) * depth]
        main += jnp.dot(some, w[chip], preferred_element_type=jnp.float32)
        some = tail[:, columns_of(chip, core, depth)]
        edge += jnp.dot(some, w[chip], preferred_element_type=jnp.float32)
    return main, edge


def partial_kernel(core, hidden, tail, w, total, rest, held, arrived):
    chips, depth, size = w.shape
    moved(
        [
            (hidden.at[:, columns_of(chip, side, depth)], to.at[:, pl.ds(chip * depth, depth)])
            for side, to in ((core[0], held), (1 - core[0], rest))
            for chip in range(chips)
        ],
        arrived,
    )
    main = jnp.zeros((hidden.shape[0], size), jnp.float32)
    edge = jnp.zeros((tail.shape[0], size), jnp.float32)
    main, edge = project(core[0], held, tail, w, main, edge)
    total[0:ROWS, :] = edge
    total[ROWS:, :] = main


def split_lanes(wide):
    high = wide.astype(jnp.bfloat16)
    low = (wide - high.astype(jnp.float32)).astype(jnp.bfloat16)
    return jnp.concatenate([high, low], axis=1)


def three_parts(wide):
    parts = []
    for _ in range(3):
        parts.append(wide.astype(jnp.bfloat16))
        wide = wide - parts[-1].astype(jnp.float32)
    return parts


def logs_of(steps):
    head_count, length = steps.shape
    earlier = lax.broadcasted_iota(jnp.int32, (length, length), 0)
    token = lax.broadcasted_iota(jnp.int32, (length, length), 1)
    upto = jnp.where(earlier <= token, 1.0, 0.0).astype(jnp.bfloat16)
    after = jnp.zeros((head_count, length), jnp.float32)
    for part in reversed(three_parts(steps)):
        after += jnp.dot(part, upto, preferred_element_type=jnp.float32)
    return after, lax.broadcasted_iota(jnp.int32, (head_count, length), 1)


def mixed_inputs(values, edge, taps, extended):
    length, channels = values.shape
    margin = taps.shape[0] - 1
    width = channels // GROUP
    extended[ROWS - margin : ROWS, :] = edge
    extended[ROWS:, :] = values[...].astype(jnp.float32)
    for part in range(GROUP):
        lanes = slice(part * width, (part + 1) * width)
        summed = jnp.zeros((length, width), jnp.float32)
        for offset in range(margin + 1):
            first = ROWS - margin + offset
            summed = (
                summed + taps[offset : offset + 1, lanes] * extended[first : first + length, lanes]
            )
        yield part, (summed * jax.nn.sigmoid(summed)).T


def weighted(mixed, weight):
    heads, length = weight.shape
    mixed = mixed.reshape(heads, mixed.shape[0] // heads, length)
    return split_lanes((mixed * weight[:, None, :]).reshape(-1, length))


def inputs_kernel(
    steps, values, before, taps, ends, end_logs, tail, extended, held, steps_held, taps_held, arrived
):
    moved([(values, held), (steps, steps_held), (taps, taps_held)], arrived)
    margin = taps.shape[0] - 1
    width = tail.shape[1]
    edge = before[...].astype(jnp.float32)
    zeros = jnp.zeros((ROWS - margin, width), jnp.float32)
    tail[...] = jnp.concatenate([zeros, edge[:, :width]], axis=0).astype(jnp.bfloat16)
    after, token = logs_of(steps_held[...])
    end_log = jnp.sum(jnp.where(token == token.shape[1] - 1, after, 0.0), axis=1, keepdims=True)
    weight = jnp.exp(end_log - after)
    end_logs[...] = jnp.broadcast_to(end_log, end_logs.shape)
    heads = weight.shape[0] // GROUP
    for part, mixed in mixed_inputs(held, edge[:, width:], taps_held, extended):
        rows = mixed.shape[0]
        some = weight[part * heads : (part + 1) * heads, :]
        ends[part * rows : (part + 1) * rows, :] = weighted(mixed, some)


def right_side(mixed_b):
    high = mixed_b.astype(jnp.bfloat16)
    low = (mixed_b - high.astype(jnp.float32)).astype(jnp.bfloat16)
    return jnp.concatenate(
        [
            jnp.concatenate([high, low], axis=1),
            jnp.concatenate([high, jnp.zeros_like(low)], axis=1),
        ],
        axis=0,
    )


def state_of(sides, right):
    both = jnp.dot(sides, right, preferred_element_type=jnp.float32)
    size = both.shape[1] // 2
    return both[:, :size] + both[:, size:]


def write_slice(sent, states, logs=None):
    heads, headdim, size = states.shape
    rows = heads * headdim // 2
    scale = scale_codes(jnp.max(jnp.abs(states), axis=1))
    sent[0:rows, :] = words_of(states * up(scale)[:, None, :]).reshape(rows, size)
    notes = scale.astype(jnp.int32)
    sent[rows:, :] = pack(notes, jnp.zeros_like(notes) if logs is None else code_logs(logs))


def read_slice(got, headdim):
    size = got.shape[1]
    half = headdim // 2
    heads = got.shape[0] // (half + 1)
    rows = heads * half
    notes = got[rows:, :]
    states = codes_of(got[0:rows, :].reshape(heads, half, size))
    return states * down(high_of(notes).astype(jnp.float32))[:, None, :], notes


def full_kernel(headdim, core, hidden, tail, w, taps, begun, ends, logs, sent, sides, extended):
    main, edge = project(1 - core[0], hidden, tail, w, begun[ROWS:, :], begun[0:ROWS, :])
    extended[0:ROWS, :] = edge
    extended[ROWS:, :] = main
    kernel = taps.shape[0]
    length, size = main.shape
    summed = jnp.zeros((length, size), jnp.float32)
    for offset in range(kernel):
        first = ROWS - kernel + 1 + offset
        summed = summed + taps[offset : offset + 1, :] * extended[first : first + length, :]
    right = right_side(summed * jax.nn.sigmoid(summed))
    sides[...] = right
    rows = ends.shape[0] // GROUP
    heads = rows // headdim
    for owner in range(GROUP):
        state = state_of(ends[owner * rows : (owner + 1) * rows, :], right)
        write_slice(
            sent.at[owner],
            state.reshape(heads, headdim, size),
            logs[owner * heads : (owner + 1) * heads, :],
        )


def kept_kernel(
    accepted, steps, values, before, taps, right, out, decay, extended, held, steps_held, taps_held, arrived
):
    moved([(values, held), (steps, steps_held), (taps, taps_held)], arrived)
    kept = accepted[0]
    after, token = logs_of(steps_held[...])
    kept_log = jnp.sum(jnp.where(token == kept - 1, after, 0.0), axis=1, keepdims=True)
    inside = token < kept
    weight = jnp.where(inside, jnp.exp(jnp.where(inside, kept_log - after, 0.0)), 0.0)
    decay[...] = jnp.broadcast_to(jnp.exp(kept_log), decay.shape)
    edge = before[...].astype(jnp.float32)[:, before.shape[1] - values.shape[1] :]
    heads = weight.shape[0] // GROUP
    for part, mixed in mixed_inputs(held, edge, taps_held, extended):
        rows = mixed.shape[0]
        some = weight[part * heads : (part + 1) * heads, :]
        out[part * rows : (part + 1) * rows, :] = state_of(weighted(mixed, some), right[...])


def group_kernel(headdim, got, prefix, decay, sent):
    rows, size = prefix.shape[1:]
    heads = rows // headdim
    half = headdim // 2
    message = half + 1
    carried = jnp.zeros((heads, headdim, size), jnp.float32)
    passed = jnp.zeros((heads, size), jnp.float32)
    for shard in range(GROUP):
        prefix[shard] = carried.reshape(rows, size)
        decay[shard] = jnp.exp(passed)
        state, notes = read_slice(got.at[shard], headdim)
        log = jnp.broadcast_to(read_logs(notes), (heads, size))
        carried = jnp.exp(log)[:, None, :] * carried + state
        passed = passed + log
    scale = scale_codes(jnp.max(jnp.abs(carried), axis=1))
    words = words_of(carried * up(scale)[:, None, :])
    for head in range(heads):
        sent[head * message : head * message + half, :] = words[head]
    sent[pl.ds(half, heads, stride=message), :] = pack(scale.astype(jnp.int32), code_logs(passed))


def scan_kernel(headdim, got, sent, held, tops, factors, decays):
    half = headdim // 2
    message = half + 1
    groups = got.shape[0] // message
    size = got.shape[1]
    notes = got[pl.ds(half, groups, stride=message), :]
    factors[...] = down(high_of(notes).astype(jnp.float32))
    decays[...] = jnp.broadcast_to(jnp.exp(read_logs(notes)), decays.shape)
    carried = jnp.zeros((headdim, size), jnp.float32)
    for group in range(groups):
        held[group * headdim : (group + 1) * headdim, :] = carried
        tops[group : group + 1, :] = jnp.max(jnp.abs(carried), axis=0, keepdims=True)
        state = codes_of(got[group * message : group * message + half, :])
        state = state * factors[group : group + 1, :]
        carried = decays[group : group + 1, :] * carried + state
    scale = scale_codes(tops[...])
    sent[pl.ds(half, groups, stride=message), :] = lax.shift_left(scale.astype(jnp.int32), 16)
    factors[...] = up(scale)
    for group in range(groups):
        scaled = held[group * headdim : (group + 1) * headdim, :] * factors[group : group + 1, :]
        sent[group * message : group * message + half, :] = words_of(scaled)


def incoming_kernel(headdim, got, prefix, decay, sent, held, factors):
    shards, rows, size = prefix.shape
    heads = rows // headdim
    half = headdim // 2
    message = half + 1
    notes = got[pl.ds(half, heads, stride=message), :]
    factors[...] = down(high_of(notes).astype(jnp.float32))
    for head in range(heads):
        state = codes_of(got[head * message : head * message + half, :])
        held[head] = state * factors[head : head + 1, :]
    for shard in range(shards):
        local = prefix[shard].reshape(heads, headdim, size)
        write_slice(sent.at[shard], decay[shard][:, None, :] * held[...] + local)


def final_kernel(headdim, got, kept, part, out):
    rows = part.shape[0] // GROUP
    size = part.shape[1]
    heads = rows // headdim
    for owner in range(GROUP):
        state, _ = read_slice(got.at[owner], headdim)
        scaled = kept[owner * heads : (owner + 1) * heads, :][:, None, :] * state
        lines = slice(owner * rows, (owner + 1) * rows)
        out[lines, :] = scaled.reshape(rows, size) + part[lines, :]


def on_device(hidden, inputs, w_b, conv_x, conv_b, log_decay, accepted):
    tokens = hidden[0]
    values = inputs[0]
    length, width = tokens.shape
    channels = values.shape[1]
    margin = conv_x.shape[0] - 1
    head_count = log_decay.shape[2]
    headdim = channels // head_count
    size = w_b.shape[1]
    message = headdim // 2 + 1
    heads = head_count // GROUP
    rows = heads * headdim
    f32, bf16, i32 = jnp.float32, jnp.bfloat16, jnp.int32
    array = jax.ShapeDtypeStruct
    shards = lax.axis_size("seq")
    parts = lax.axis_size("fsdp")
    group_count = shards // GROUP
    near = [[g * GROUP + i for i in range(GROUP)] for g in range(group_count)]
    far = [[g * GROUP + i for g in range(group_count)] for i in range(GROUP)]
    core = jnp.reshape(lax.axis_index("fsdp") % 2, (1,)).astype(i32)

    def exchange(sent, members):
        return lax.all_to_all(sent, "seq", 0, 0, axis_index_groups=members)

    def exchange_heads(sent):
        return exchange(sent.reshape(heads, 1, message * size), far).reshape(sent.shape)

    chips = [[i for i in range(parts) if i % 2 == c] for c in range(2)]
    w_copies = copies(w_b, parts // 2)
    w_own = lax.all_to_all(w_copies, "fsdp", 0, 0, axis_index_groups=chips)
    dma = pltpu.SemaphoreType.DMA
    edge = call(
        edge_kernel,
        tokens,
        values,
        far=(0, 1),
        out=array((margin, width + channels), bf16),
        scratch=[pltpu.VMEM((ROWS, width), bf16), pltpu.VMEM((ROWS, channels), bf16), dma((2,))],
    )
    before = lax.ppermute(edge, "seq", [(i, i + 1) for i in range(shards - 1)])

    steps = log_decay[0].T
    wide = array((head_count, size), f32)
    scratch = [
        pltpu.VMEM((ROWS + length, channels), f32),
        pltpu.VMEM(values.shape, values.dtype),
        pltpu.VMEM(steps.shape, f32),
        pltpu.VMEM(conv_x.shape, f32),
        dma((3,)),
    ]
    ends_x, end_logs, tail = call(
        inputs_kernel,
        steps,
        values,
        before,
        conv_x,
        far=(0, 1, 3),
        out=[array((channels, 2 * length), bf16), wide, array((ROWS, width), bf16)],
        scratch=scratch,
    )

    w_own, before = lax.optimization_barrier((w_own, before))
    w_other = lax.ppermute(w_own, "fsdp", [(i, i ^ 1) for i in range(parts)])
    begun, rest = call(
        partial_kernel,
        core,
        tokens,
        tail,
        w_own,
        far=(1,),
        out=[array((ROWS + length, size), f32), array((length, width // 2), bf16)],
        scratch=[pltpu.VMEM((length, width // 2), bf16), dma((parts,))],
    )

    slices = array((GROUP, heads * message, size), i32)
    sent, right = call(
        functools.partial(full_kernel, headdim),
        core,
        rest,
        tail,
        w_other,
        conv_b,
        begun,
        ends_x,
        end_logs,
        out=[slices, array((2 * length, 2 * size), bf16)],
        scratch=[pltpu.VMEM((ROWS + length, size), f32)],
    )
    prefix, decay, sent = call(
        functools.partial(group_kernel, headdim),
        exchange(sent, near),
        out=[
            array((GROUP, rows, size), f32),
            array((GROUP, heads, size), f32),
            array((heads * message, size), i32),
        ],
    )
    part, kept_decay = call(
        kept_kernel,
        accepted[0],
        steps,
        values,
        before,
        conv_x,
        right,
        far=(1, 2, 4),
        out=[array((channels, size), f32), wide],
        scratch=scratch,
    )

    sent = call(
        functools.partial(scan_kernel, headdim),
        exchange_heads(sent),
        out=array(sent.shape, i32),
        scratch=[pltpu.VMEM((group_count * headdim, size), f32)]
        + [pltpu.VMEM((group_count, size), f32)] * 3,
    )
    sent = call(
        functools.partial(incoming_kernel, headdim),
        exchange_heads(sent),
        prefix,
        decay,
        out=slices,
        scratch=[pltpu.VMEM((heads, headdim, size), f32), pltpu.VMEM((heads, size), f32)],
    )
    final = call(
        functools.partial(final_kernel, headdim),
        exchange(sent, near),
        kept_decay,
        part,
        out=array((channels, size), f32),
    )
    return final.reshape(1, 1, head_count, headdim, size)


def solution(mesh):
    placed = (
        P("fsdp", "seq", None),
        P("fsdp", "seq", None),
        P("fsdp", None),
        P(),
        P(),
        P("fsdp", "seq", None),
        P("fsdp", "seq"),
    )
    return jax.shard_map(
        on_device,
        mesh=mesh,
        in_specs=placed,
        out_specs=P("fsdp", "seq", None, None, None),
        check_vma=False,
    )
```

time: 665 us -> 114 us (0.17)
  the two profiles are of different devices: /device:TPU:504 before, /device:TPU:1 now
where the time goes in v2:
time: 114 us; the launch traced here: 112 us
  blocking collectives  66 us (58%)
  starting transfers between devices  21.7 us (19%)
  waiting for transfers between devices  13.7 us (12%)
  Pallas kernels  8.58 us (8%)
    all_to_all x3, blocking collectives, exchange(): return lax.all_to_all(sent, 'seq', 0, 0, axis_index_groups=members)  66 us
    all_to_all x1, waiting for transfers between devices, exchange(): return lax.all_to_all(sent, 'seq', 0, 0, axis_index_groups=members)  10 us
    ppermute x1, starting transfers between devices, on_device(): w_other = lax.ppermute(w_own, 'fsdp', [(i, i ^ 1) for i in range(parts)])  8.54 us
    pallas_call x9, Pallas kernels, call(): pl.pallas_call(kernel, in_specs=[pl.BlockSpec(memory_space=place) for pla...  7.54 us
    all_to_all x1, starting transfers between devices, on_device(): w_own = lax.all_to_all(w_copies, 'fsdp', 0, 0, axis_index_groups=chips)  4.85 us
    all_to_all x1, starting transfers between devices, exchange(): return lax.all_to_all(sent, 'seq', 0, 0, axis_index_groups=members)  4.77 us
    ppermute x1, starting transfers between devices, on_device(): before = lax.ppermute(edge, 'seq', [(i, i + 1) for i in range(shards - 1)])  3.54 us
    all_to_all x1, waiting for transfers between devices, on_device(): w_own = lax.all_to_all(w_copies, 'fsdp', 0, 0, axis_index_groups=chips)  2.5 us
  transfers between devices with their start and end apart: 4, of which 3 were waited for; matrix products, arithmetic and copies ran while one was open for 0% of the time, Pallas kernels for 3%

profile of v2, /device:TPU:1, one launch (start us, length us, event | category | flops | bytes accessed | tf_op | source)
XLA Modules:
  0.0 111.9 jit_solution(11480024132595307832)
XLA Ops:
  0.0 0.0 copy-start.1
  0.0 0.0 copy-start
  0.0 1.0 copy-done.2
  1.1 1.0 shard_map.75
  2.1 0.0 copy-start.3
  2.1 0.0 copy-start.4
  2.1 4.9 %all-to-all-start = ((bf16[4,640,128]{2,1,0:T(8,128)(2,1)}), bf16[4,640,128]{2,1,0:T(8,128)(2,1)S(1)}, u32[]{:S(2)}, u32[]{:S(2)}) async-start(bf16[4,640,128]{2,1,0:T(8,128)(2,1)} %shard_map.75), calls=%async_computation | async-start | bytes 1310720 | tf_op jit(solution)/shard_map/all_to_all | solution.py:393
  7.0 0.0 copy-done.1
  7.0 0.0 copy-done
  7.0 0.3 shard_map.73
  7.3 3.5 %collective-permute-start = (bf16[3,7168]{1,0:T(4,128)(2,1)S(1)}, bf16[3,7168]{1,0:T(4,128)(2,1)S(1)}, u32[]{:S(2)}, u32[]{:S(2)}) collective-permute-start(bf16[3,7168]{1,0:T(4,128)(2,1)S(1)} %shard_map.73), channel_id=1, source_target_pairs={{0,8},{8,16},{16,24},{24,32},{32,40},{40,48},{48,56},{56,64},{64,7... | collective-permute-start | bytes 129032 | tf_op jit(solution)/shard_map/ppermute | solution.py:403
  10.9 1.2 %collective-permute-done.before = bf16[3,7168]{1,0:T(4,128)(2,1)S(1)} collective-permute-done((bf16[3,7168]{1,0:T(4,128)(2,1)S(1)}, bf16[3,7168]{1,0:T(4,128)(2,1)S(1)}, u32[]{:S(2)}, u32[]{:S(2)}) %collective-permute-start) | collective-permute-done | bytes 43040 | tf_op jit(solution)/shard_map/ppermute | solution.py:403
  12.1 2.5 %all-to-all-done.w = bf16[4,640,128]{2,1,0:T(8,128)(2,1)S(1)} async-done(((bf16[4,640,128]{2,1,0:T(8,128)(2,1)}), bf16[4,640,128]{2,1,0:T(8,128)(2,1)S(1)}, u32[]{:S(2)}, u32[]{:S(2)}) %all-to-all-start) | async-done | bytes 655392 | tf_op jit(solution)/shard_map/all_to_all | solution.py:393
  14.6 8.5 %collective-permute-start.1 = (bf16[4,640,128]{2,1,0:T(8,128)(2,1)S(1)}, bf16[4,640,128]{2,1,0:T(8,128)(2,1)S(1)}, u32[]{:S(2)}, u32[]{:S(2)}) collective-permute-start(bf16[4,640,128]{2,1,0:T(8,128)(2,1)S(1)} %all-to-all-done.w), channel_id=1, source_target_pairs={{0,1},{1,0},{2,3},{3,2},{4,5},{5,4},{6,7},{7,6},{8,9},{9,8},{10,11... | collective-permute-start | bytes 1966088 | tf_op jit(solution)/shard_map/ppermute | solution.py:426
  23.2 0.0 copy-done.3
  23.2 0.0 copy-done.4
  23.2 0.0 copy-start.5
  23.2 1.2 %shard_map.74 = (bf16[2048,256]{1,0:T(8,128)(2,1)S(1)}, f32[64,128]{1,0:T(8,128)S(1)}, bf16[16,5120]{1,0:T(8,128)(2,1)S(1)}) custom-call(f32[64,128]{1,0:T(8,128)S(1)} %bitcast.22, bf16[128,2048]{1,0:T(8,128)(2,1)S(1)} %bitcast.16, bf16[3,7168]{1,0:T(4,128)(2,1)S(1)} %collective-permute-done.before, f32[4,2048]{1,0:T(4,128)S(1)} %copy-done.4), custom_call_target="tpu_custom_call" | custom-call | tf_op jit(solution)/shard_map/pallas_call | solution.py:23
  24.4 0.7 shard_map.76
  25.1 0.0 collective-permute-done.1.w
  25.1 0.0 copy-done.5
  25.1 1.0 shard_map.77
  26.2 17.8 %all_to_all.25.got = s32[4,272,128]{2,1,0:T(8,128)S(1)} all-to-all(s32[4,272,128]{2,1,0:T(8,128)S(1)} %get-tuple-element.25), channel_id=1, replica_groups={{0,8,16,24},{32,40,48,56},{64,72,80,88},{96,104,112,120},{128,136,144,1..., dimensions={0} | all-to-all | bytes 1114112 | tf_op jit(solution)/shard_map/all_to_all | solution.py:386
  44.0 0.3 shard_map.78
  44.3 30.8 %all_to_all.26 = s32[16,1,2176]{2,1,0:T(1,128)S(1)} all-to-all(s32[16,1,2176]{2,1,0:T(1,128)S(1)} %bitcast.21), channel_id=1, replica_groups={{0,32,64,96,128,160,192,224,256,288,320,352,384,416,448,480},{8,40,72,1..., dimensions={0} | all-to-all | bytes 278528 | tf_op jit(solution)/shard_map/all_to_all | solution.py:386
  75.2 0.2 shard_map.79
  75.4 17.3 %all_to_all.27 = s32[16,1,2176]{2,1,0:T(1,128)S(1)} all-to-all(s32[16,1,2176]{2,1,0:T(1,128)S(1)} %bitcast.20), channel_id=1, replica_groups={{0,32,64,96,128,160,192,224,256,288,320,352,384,416,448,480},{8,40,72,1..., dimensions={0} | all-to-all | bytes 278528 | tf_op jit(solution)/shard_map/all_to_all | solution.py:386
  92.7 1.2 %shard_map.80 = s32[4,272,128]{2,1,0:T(8,128)} custom-call(s32[272,128]{1,0:T(8,128)S(1)} %bitcast.18, f32[4,512,128]{2,1,0:T(8,128)S(1)} %get-tuple-element.27.prefix, f32[4,16,128]{2,1,0:T(8,128)S(1)} %get-tuple-element.28.decay), custom_call_target="tpu_custom_call" | custom-call | tf_op jit(solution)/shard_map/pallas_call | solution.py:23
  93.9 4.8 %all-to-all-start.4 = ((s32[4,272,128]{2,1,0:T(8,128)}), s32[4,272,128]{2,1,0:T(8,128)S(1)}, u32[]{:S(2)}, u32[]{:S(2)}) async-start(s32[4,272,128]{2,1,0:T(8,128)} %shard_map.80), calls=%async_computation.4 | async-start | bytes 1114112 | tf_op jit(solution)/shard_map/all_to_all | solution.py:386
  99.3 1.3 %shard_map.81 = (f32[2048,128]{1,0:T(8,128)S(1)}, f32[64,128]{1,0:T(8,128)S(1)}) custom-call(s32[1]{0:T(128)} %bitcast.12.accepted, f32[64,128]{1,0:T(8,128)S(1)} %bitcast.23, bf16[128,2048]{1,0:T(8,128)(2,1)S(1)} %bitcast.17, bf16[3,7168]{1,0:T(4,128)(2,1)S(1)} %collective-permute-done.before, f32[4,2048]{1,0:T(4,128)S(1)} %copy-done.4, ...), custom_call_target="tpu_custom_call" | custom-call | tf_op jit(solution)/shard_map/pallas_call | solution.py:23
  100.7 10.0 %all-to-all-done.4.got = s32[4,272,128]{2,1,0:T(8,128)S(1)} async-done(((s32[4,272,128]{2,1,0:T(8,128)}), s32[4,272,128]{2,1,0:T(8,128)S(1)}, u32[]{:S(2)}, u32[]{:S(2)}) %all-to-all-start.4) | async-done | bytes 557088 | tf_op jit(solution)/shard_map/all_to_all | solution.py:386
  110.7 1.2 %shard_map.82 = f32[2048,128]{1,0:T(8,128)} custom-call(s32[4,272,128]{2,1,0:T(8,128)S(1)} %all-to-all-done.4.got, f32[64,128]{1,0:T(8,128)S(1)} %get-tuple-element.31.kept, f32[2048,128]{1,0:T(8,128)S(1)} %get-tuple-element.32.part), custom_call_target="tpu_custom_call" | custom-call | tf_op jit(solution)/shard_map/pallas_call | solution.py:23
  (1 shorter events, 0.0 us)
Async XLA Ops:
  0.0 7.0 %copy-start.1 = (bf16[1,128,2048]{2,1,0:T(8,128)(2,1)S(1)}, bf16[1,128,2048]{2,1,0:T(8,128)(2,1)}, u32[]{:S(2)}) copy-start(bf16[1,128,2048]{2,1,0:T(8,128)(2,1)} %param.8) | copy-start | bytes 1572868
  0.0 7.0 %copy-start = (bf16[1,128,5120]{2,1,0:T(8,128)(2,1)S(1)}, bf16[1,128,5120]{2,1,0:T(8,128)(2,1)}, u32[]{:S(2)}) copy-start(bf16[1,128,5120]{2,1,0:T(8,128)(2,1)} %param.7) | copy-start | bytes 3932164
  0.0 1.1 copy-start.2
  2.1 21.1 %copy-start.3 = (f32[1,128,64]{1,2,0:T(8,128)S(1)}, f32[1,128,64]{1,2,0:T(8,128)}, u32[]{:S(2)}) copy-start(f32[1,128,64]{1,2,0:T(8,128)} %param.12) | copy-start | bytes 98308
  2.1 21.1 %copy-start.4 = (f32[4,2048]{1,0:T(4,128)S(1)}, f32[4,2048]{1,0:T(4,128)}, u32[]{:S(2)}) copy-start(f32[4,2048]{1,0:T(4,128)} %taps.5) | copy-start | bytes 98308
  2.1 12.5 %all-to-all-start = ((bf16[4,640,128]{2,1,0:T(8,128)(2,1)}), bf16[4,640,128]{2,1,0:T(8,128)(2,1)S(1)}, u32[]{:S(2)}, u32[]{:S(2)}) async-start(bf16[4,640,128]{2,1,0:T(8,128)(2,1)} %shard_map.75), calls=%async_computation | async-start | bytes 1310720 | tf_op jit(solution)/shard_map/all_to_all | solution.py:393
  7.3 4.8 %collective-permute-start = (bf16[3,7168]{1,0:T(4,128)(2,1)S(1)}, bf16[3,7168]{1,0:T(4,128)(2,1)S(1)}, u32[]{:S(2)}, u32[]{:S(2)}) collective-permute-start(bf16[3,7168]{1,0:T(4,128)(2,1)S(1)} %shard_map.73), channel_id=1, source_target_pairs={{0,8},{8,16},{16,24},{24,32},{32,40},{40,48},{48,56},{56,64},{64,7... | collective-permute-start | bytes 129032 | tf_op jit(solution)/shard_map/ppermute | solution.py:403
  14.6 10.5 %collective-permute-start.1 = (bf16[4,640,128]{2,1,0:T(8,128)(2,1)S(1)}, bf16[4,640,128]{2,1,0:T(8,128)(2,1)S(1)}, u32[]{:S(2)}, u32[]{:S(2)}) collective-permute-start(bf16[4,640,128]{2,1,0:T(8,128)(2,1)S(1)} %all-to-all-done.w), channel_id=1, source_target_pairs={{0,1},{1,0},{2,3},{3,2},{4,5},{5,4},{6,7},{7,6},{8,9},{9,8},{10,11... | collective-permute-start | bytes 1966088 | tf_op jit(solution)/shard_map/ppermute | solution.py:426
  23.2 1.9 %copy-start.5 = (f32[4,128]{1,0:T(4,128)S(1)}, f32[4,128]{1,0:T(4,128)}, u32[]{:S(2)}) copy-start(f32[4,128]{1,0:T(4,128)} %taps.4) | copy-start | bytes 6148
  93.9 16.8 %all-to-all-start.4 = ((s32[4,272,128]{2,1,0:T(8,128)}), s32[4,272,128]{2,1,0:T(8,128)S(1)}, u32[]{:S(2)}, u32[]{:S(2)}) async-start(s32[4,272,128]{2,1,0:T(8,128)} %shard_map.80), calls=%async_computation.4 | async-start | bytes 1114112 | tf_op jit(solution)/shard_map/all_to_all | solution.py:386

commit v3 on v2

--- a/solution.py
+++ b/solution.py
@@ -9,13 +9,14 @@
 
 ROWS = 16
 GROUP = 4
+SHIFT = 2
 TOP = 32760.0
 FINE = 128.0
 LOG_STEP = float(2**19)
 VMEM = 12 * 1024 * 1024
 
 
-def call(kernel, *args, out, scratch=(), far=()):
+def call(kernel, *args, out, scratch=(), far=(), out_space=pltpu.VMEM):
     places = [
         pltpu.SMEM if a.shape == (1,) else pltpu.HBM if i in far else pltpu.VMEM
         for i, a in enumerate(args)
@@ -23,7 +24,7 @@
     return pl.pallas_call(
         kernel,
         in_specs=[pl.BlockSpec(memory_space=place) for place in places],
-        out_specs=jax.tree.map(lambda _: pl.BlockSpec(memory_space=pltpu.VMEM), out),
+        out_specs=jax.tree.map(lambda _: pl.BlockSpec(memory_space=out_space), out),
         out_shape=out,
         scratch_shapes=scratch,
         compiler_params=pltpu.CompilerParams(vmem_limit_bytes=VMEM),
@@ -90,18 +91,17 @@
         move.wait()
 
 
-def copies_kernel(w, out, held, arrived):
-    moved([(w, held)], arrived)
-    moved([(held, out.at[copy]) for copy in range(out.shape[0])], arrived)
+def copies_kernel(w, out, arrived):
+    moved([(w, out.at[copy]) for copy in range(out.shape[0])], arrived)
 
 
 def copies(w, count):
     return pl.pallas_call(
         copies_kernel,
-        in_specs=[pl.BlockSpec(memory_space=pltpu.HBM)],
+        in_specs=[pl.BlockSpec(memory_space=pltpu.VMEM)],
         out_specs=pl.BlockSpec(memory_space=pltpu.HBM),
         out_shape=jax.ShapeDtypeStruct((count, *w.shape), w.dtype),
-        scratch_shapes=[pltpu.VMEM(w.shape, w.dtype), pltpu.SemaphoreType.DMA((count,))],
+        scratch_shapes=[pltpu.SemaphoreType.DMA((count,))],
         compiler_params=pltpu.CompilerParams(vmem_limit_bytes=VMEM),
     )(w)
 
@@ -291,7 +291,8 @@
         out[part * rows : (part + 1) * rows, :] = state_of(weighted(mixed, some), right[...])
 
 
-def group_kernel(headdim, got, prefix, decay, sent):
+def group_kernel(headdim, wraps, got, prefix, decay, sent):
+    goes_on = jnp.where(wraps[0] > 0, 0.0, 1.0)
     rows, size = prefix.shape[1:]
     heads = rows // headdim
     half = headdim // 2
@@ -299,8 +300,11 @@
     carried = jnp.zeros((heads, headdim, size), jnp.float32)
     passed = jnp.zeros((heads, size), jnp.float32)
     for shard in range(GROUP):
+        if shard == SHIFT:
+            carried = carried * goes_on
+            passed = passed * goes_on
         prefix[shard] = carried.reshape(rows, size)
-        decay[shard] = jnp.exp(passed)
+        decay[shard] = jnp.exp(passed) * (goes_on if shard >= SHIFT else 1.0)
         state, notes = read_slice(got.at[shard], headdim)
         log = jnp.broadcast_to(read_logs(notes), (heads, size))
         carried = jnp.exp(log)[:, None, :] * carried + state
@@ -312,7 +316,7 @@
     sent[pl.ds(half, heads, stride=message), :] = pack(scale.astype(jnp.int32), code_logs(passed))
 
 
-def scan_kernel(headdim, got, sent, held, tops, factors, decays):
+def scan_kernel(headdim, core, got, sent, held, tops, factors, decays):
     half = headdim // 2
     message = half + 1
     groups = got.shape[0] // message
@@ -320,7 +324,8 @@
     notes = got[pl.ds(half, groups, stride=message), :]
     factors[...] = down(high_of(notes).astype(jnp.float32))
     decays[...] = jnp.broadcast_to(jnp.exp(read_logs(notes)), decays.shape)
-    carried = jnp.zeros((headdim, size), jnp.float32)
+    first = codes_of(got[(groups - 1) * message : (groups - 1) * message + half, :])
+    carried = first * factors[groups - 1 : groups, :] * jnp.where(core[0] > 0, 1.0, 0.0)
     for group in range(groups):
         held[group * headdim : (group + 1) * headdim, :] = carried
         tops[group : group + 1, :] = jnp.max(jnp.abs(carried), axis=0, keepdims=True)
@@ -335,7 +340,7 @@
         sent[group * message : group * message + half, :] = words_of(scaled)
 
 
-def incoming_kernel(headdim, got, prefix, decay, sent, held, factors):
+def incoming_kernel(headdim, got, prefix, decay, sent, held, factors, staged, arrived):
     shards, rows, size = prefix.shape
     heads = rows // headdim
     half = headdim // 2
@@ -347,18 +352,29 @@
         held[head] = state * factors[head : head + 1, :]
     for shard in range(shards):
         local = prefix[shard].reshape(heads, headdim, size)
-        write_slice(sent.at[shard], decay[shard][:, None, :] * held[...] + local)
-
-
-def final_kernel(headdim, got, kept, part, out):
+        write_slice(staged.at[shard], decay[shard][:, None, :] * held[...] + local)
+        pltpu.make_async_copy(staged.at[shard], sent.at[shard], arrived.at[shard]).start()
+    for shard in range(shards):
+        pltpu.make_async_copy(staged.at[shard], sent.at[shard], arrived.at[shard]).wait()
+
+
+def final_kernel(headdim, got, kept, part, out, staged, arrived):
     rows = part.shape[0] // GROUP
     size = part.shape[1]
     heads = rows // headdim
+    moves = []
     for owner in range(GROUP):
         state, _ = read_slice(got.at[owner], headdim)
         scaled = kept[owner * heads : (owner + 1) * heads, :][:, None, :] * state
         lines = slice(owner * rows, (owner + 1) * rows)
-        out[lines, :] = scaled.reshape(rows, size) + part[lines, :]
+        staged[lines, :] = scaled.reshape(rows, size) + part[lines, :]
+        lines = pl.ds(owner * rows, rows)
+        moves.append(
+            pltpu.make_async_copy(staged.at[lines, :], out.at[lines, :], arrived.at[owner])
+        )
+        moves[-1].start()
+    for move in moves:
+        move.wait()
 
 
 def on_device(hidden, inputs, w_b, conv_x, conv_b, log_decay, accepted):
@@ -378,12 +394,28 @@
     shards = lax.axis_size("seq")
     parts = lax.axis_size("fsdp")
     group_count = shards // GROUP
-    near = [[g * GROUP + i for i in range(GROUP)] for g in range(group_count)]
-    far = [[g * GROUP + i for g in range(group_count)] for i in range(GROUP)]
-    core = jnp.reshape(lax.axis_index("fsdp") % 2, (1,)).astype(i32)
+
+    def device(side, part, place):
+        return (place + SHIFT * side) % shards * parts + 2 * part + side
+
+    sides = [(side, part) for part in range(parts // 2) for side in range(2)]
+    near = [
+        [device(side, part, group * GROUP + i) for i in range(GROUP)]
+        for side, part in sides
+        for group in range(group_count)
+    ]
+    far = [
+        [device(side, part, group * GROUP + i) for group in range(group_count)]
+        for side, part in sides
+        for i in range(GROUP)
+    ]
+    core = lax.axis_index("fsdp") % 2
+    place = (lax.axis_index("seq") - SHIFT * core) % shards
+    wraps = jnp.reshape(core * (place // GROUP == group_count - 1), (1,)).astype(i32)
+    core = jnp.reshape(core, (1,)).astype(i32)
 
     def exchange(sent, members):
-        return lax.all_to_all(sent, "seq", 0, 0, axis_index_groups=members)
+        return lax.all_to_all(sent, ("seq", "fsdp"), 0, 0, axis_index_groups=members)
 
     def exchange_heads(sent):
         return exchange(sent.reshape(heads, 1, message * size), far).reshape(sent.shape)
@@ -451,6 +483,7 @@
     )
     prefix, decay, sent = call(
         functools.partial(group_kernel, headdim),
+        wraps,
         exchange(sent, near),
         out=[
             array((GROUP, rows, size), f32),
@@ -473,6 +506,7 @@
 
     sent = call(
         functools.partial(scan_kernel, headdim),
+        core,
         exchange_heads(sent),
         out=array(sent.shape, i32),
         scratch=[pltpu.VMEM((group_count * headdim, size), f32)]
@@ -484,7 +518,13 @@
         prefix,
         decay,
         out=slices,
-        scratch=[pltpu.VMEM((heads, headdim, size), f32), pltpu.VMEM((heads, size), f32)],
+        out_space=pltpu.HBM,
+        scratch=[
+            pltpu.VMEM((heads, headdim, size), f32),
+            pltpu.VMEM((heads, size), f32),
+            pltpu.VMEM(slices.shape, i32),
+            dma((GROUP,)),
+        ],
     )
     final = call(
         functools.partial(final_kernel, headdim),
@@ -492,6 +532,8 @@
         kept_decay,
         part,
         out=array((channels, size), f32),
+        out_space=pltpu.HBM,
+        scratch=[pltpu.VMEM((channels, size), f32), dma((GROUP,))],
     )
     return final.reshape(1, 1, head_count, headdim, size)
 

time: 114 us -> 113 us (level)
  the two profiles are of different devices: /device:TPU:1 before, /device:TPU:32 now
where the time goes in v3:
time: 113 us; the launch traced here: 112 us
  blocking collectives  52.6 us (47%)
  waiting for transfers between devices  29.2 us (26%)
  starting transfers between devices  19.5 us (17%)
  Pallas kernels  8.99 us (8%)
    all_to_all x2, blocking collectives, exchange(): lax.all_to_all(sent, ('seq', 'fsdp'), 0, 0, axis_index_groups=members)  52.6 us
    all_to_all x2, waiting for transfers between devices, exchange(): lax.all_to_all(sent, ('seq', 'fsdp'), 0, 0, axis_index_groups=members)  22.4 us
    all_to_all x2, starting transfers between devices, exchange(): lax.all_to_all(sent, ('seq', 'fsdp'), 0, 0, axis_index_groups=members)  9.48 us
    pallas_call x9, Pallas kernels, call(): pl.pallas_call(kernel, in_specs=[pl.BlockSpec(memory_space=place) for pla...  8.13 us
    all_to_all x1, starting transfers between devices, on_device(): w_own = lax.all_to_all(w_copies, 'fsdp', 0, 0, axis_index_groups=chips)  4.3 us
    ppermute x1, waiting for transfers between devices, on_device(): before = lax.ppermute(edge, 'seq', [(i, i + 1) for i in range(shards - 1)])  4.3 us
    ppermute x1, starting transfers between devices, on_device(): before = lax.ppermute(edge, 'seq', [(i, i + 1) for i in range(shards - 1)])  3.83 us
    all_to_all x1, waiting for transfers between devices, on_device(): w_own = lax.all_to_all(w_copies, 'fsdp', 0, 0, axis_index_groups=chips)  2.4 us
  transfers between devices with their start and end apart: 5, of which 5 were waited for; matrix products, arithmetic and copies ran while one was open for 0% of the time, Pallas kernels for 3%

profile of v3, /device:TPU:32, one launch (start us, length us, event | category | flops | bytes accessed | tf_op | source)
XLA Modules:
  0.0 112.2 jit_solution(15687226267822876291)
XLA Ops:
  0.0 0.0 copy-start
  0.0 1.0 copy-done.2
  1.1 0.9 shard_map.75
  1.9 0.0 copy-start.3
  1.9 0.0 copy-start.4
  1.9 4.3 %all-to-all-start = ((bf16[4,640,128]{2,1,0:T(8,128)(2,1)}), bf16[4,640,128]{2,1,0:T(8,128)(2,1)S(1)}, u32[]{:S(2)}, u32[]{:S(2)}) async-start(bf16[4,640,128]{2,1,0:T(8,128)(2,1)} %shard_map.75), calls=%async_computation | async-start | bytes 1310720 | tf_op jit(solution)/shard_map/all_to_all | solution.py:425
  6.3 0.0 copy-done.1
  6.3 0.0 copy-done
  6.3 0.3 shard_map.73
  6.6 3.8 %collective-permute-start = (bf16[3,7168]{1,0:T(4,128)(2,1)S(1)}, bf16[3,7168]{1,0:T(4,128)(2,1)S(1)}, u32[]{:S(2)}, u32[]{:S(2)}) collective-permute-start(bf16[3,7168]{1,0:T(4,128)(2,1)S(1)} %shard_map.73), channel_id=1, source_target_pairs={{0,8},{8,16},{16,24},{24,32},{32,40},{40,48},{48,56},{56,64},{64,7... | collective-permute-start | bytes 129032 | tf_op jit(solution)/shard_map/ppermute | solution.py:435
  10.4 4.3 %collective-permute-done.before = bf16[3,7168]{1,0:T(4,128)(2,1)S(1)} collective-permute-done((bf16[3,7168]{1,0:T(4,128)(2,1)S(1)}, bf16[3,7168]{1,0:T(4,128)(2,1)S(1)}, u32[]{:S(2)}, u32[]{:S(2)}) %collective-permute-start) | collective-permute-done | bytes 43040 | tf_op jit(solution)/shard_map/ppermute | solution.py:435
  14.7 2.4 %all-to-all-done.w = bf16[4,640,128]{2,1,0:T(8,128)(2,1)S(1)} async-done(((bf16[4,640,128]{2,1,0:T(8,128)(2,1)}), bf16[4,640,128]{2,1,0:T(8,128)(2,1)S(1)}, u32[]{:S(2)}, u32[]{:S(2)}) %all-to-all-start) | async-done | bytes 655392 | tf_op jit(solution)/shard_map/all_to_all | solution.py:425
  17.1 1.9 %collective-permute-start.1 = (bf16[4,640,128]{2,1,0:T(8,128)(2,1)S(1)}, bf16[4,640,128]{2,1,0:T(8,128)(2,1)S(1)}, u32[]{:S(2)}, u32[]{:S(2)}) collective-permute-start(bf16[4,640,128]{2,1,0:T(8,128)(2,1)S(1)} %all-to-all-done.w), channel_id=1, source_target_pairs={{0,1},{1,0},{2,3},{3,2},{4,5},{5,4},{6,7},{7,6},{8,9},{9,8},{10,11... | collective-permute-start | bytes 1966088 | tf_op jit(solution)/shard_map/ppermute | solution.py:458
  19.1 0.0 copy-done.3
  19.1 0.0 copy-done.4
  19.1 0.0 copy-start.5
  19.1 1.2 %shard_map.74 = (bf16[2048,256]{1,0:T(8,128)(2,1)S(1)}, f32[64,128]{1,0:T(8,128)S(1)}, bf16[16,5120]{1,0:T(8,128)(2,1)S(1)}) custom-call(f32[64,128]{1,0:T(8,128)S(1)} %bitcast.23, bf16[128,2048]{1,0:T(8,128)(2,1)S(1)} %bitcast.17, bf16[3,7168]{1,0:T(4,128)(2,1)S(1)} %collective-permute-done.before, f32[4,2048]{1,0:T(4,128)S(1)} %copy-done.4), custom_call_target="tpu_custom_call" | custom-call | tf_op jit(solution)/shard_map/pallas_call | solution.py:24
  20.3 0.7 shard_map.76
  21.0 0.1 collective-permute-done.1.w
  21.1 0.0 copy-done.5
  21.1 1.8 %shard_map.77 = (s32[4,272,128]{2,1,0:T(8,128)}, bf16[256,256]{1,0:T(8,128)(2,1)S(1)}) custom-call(s32[1]{0:T(128)} %bitcast.core, bf16[128,2560]{1,0:T(8,128)(2,1)S(1)} %get-tuple-element.21.hidden, bf16[16,5120]{1,0:T(8,128)(2,1)S(1)} %get-tuple-element.19.tail, bf16[4,640,128]{2,1,0:T(8,128)(2,1)S(1)} %collective-permute-done.1.w, ...), custom_call_target="tpu_custom_call" | custom-call | tf_op jit(solution)/shard_map/pallas_call | solution.py:24
  23.0 6.0 %all-to-all-start.1 = ((s32[4,272,128]{2,1,0:T(8,128)}), s32[4,272,128]{2,1,0:T(8,128)S(1)}, u32[]{:S(2)}, u32[]{:S(2)}) async-start(s32[4,272,128]{2,1,0:T(8,128)} %get-tuple-element.25), calls=%async_computation.1 | async-start | bytes 1114112 | tf_op jit(solution)/shard_map/all_to_all | solution.py:418
  29.0 13.1 %all-to-all-done.1.got = s32[4,272,128]{2,1,0:T(8,128)S(1)} async-done(((s32[4,272,128]{2,1,0:T(8,128)}), s32[4,272,128]{2,1,0:T(8,128)S(1)}, u32[]{:S(2)}, u32[]{:S(2)}) %all-to-all-start.1) | async-done | bytes 557088 | tf_op jit(solution)/shard_map/all_to_all | solution.py:418
  42.1 0.3 shard_map.78
  42.4 31.2 %all_to_all.25 = s32[16,1,2176]{2,1,0:T(1,128)S(1)} all-to-all(s32[16,1,2176]{2,1,0:T(1,128)S(1)} %bitcast.22), channel_id=1, replica_groups={{0,32,64,96,128,160,192,224,256,288,320,352,384,416,448,480},{8,40,72,1..., dimensions={0} | all-to-all | bytes 278528 | tf_op jit(solution)/shard_map/all_to_all | solution.py:418
  73.6 0.2 shard_map.79
  73.8 21.4 %all_to_all.26 = s32[16,1,2176]{2,1,0:T(1,128)S(1)} all-to-all(s32[16,1,2176]{2,1,0:T(1,128)S(1)} %bitcast.21), channel_id=1, replica_groups={{0,32,64,96,128,160,192,224,256,288,320,352,384,416,448,480},{8,40,72,1..., dimensions={0} | all-to-all | bytes 278528 | tf_op jit(solution)/shard_map/all_to_all | solution.py:418
  95.2 1.2 %shard_map.80 = s32[4,272,128]{2,1,0:T(8,128)} custom-call(s32[272,128]{1,0:T(8,128)S(1)} %bitcast.19, f32[4,512,128]{2,1,0:T(8,128)S(1)} %get-tuple-element.27.prefix, f32[4,16,128]{2,1,0:T(8,128)S(1)} %get-tuple-element.28.decay), custom_call_target="tpu_custom_call" | custom-call | tf_op jit(solution)/shard_map/pallas_call | solution.py:24
  96.3 3.5 %all-to-all-start.4 = ((s32[4,272,128]{2,1,0:T(8,128)}), s32[4,272,128]{2,1,0:T(8,128)S(1)}, u32[]{:S(2)}, u32[]{:S(2)}) async-start(s32[4,272,128]{2,1,0:T(8,128)} %shard_map.80), calls=%async_computation.4 | async-start | bytes 1114112 | tf_op jit(solution)/shard_map/all_to_all | solution.py:418
  100.5 1.3 %shard_map.81 = (f32[2048,128]{1,0:T(8,128)S(1)}, f32[64,128]{1,0:T(8,128)S(1)}) custom-call(s32[1]{0:T(128)} %bitcast.13.accepted, f32[64,128]{1,0:T(8,128)S(1)} %bitcast.24, bf16[128,2048]{1,0:T(8,128)(2,1)S(1)} %bitcast.18, bf16[3,7168]{1,0:T(4,128)(2,1)S(1)} %collective-permute-done.before, f32[4,2048]{1,0:T(4,128)S(1)} %copy-done.4, ...), custom_call_target="tpu_custom_call" | custom-call | tf_op jit(solution)/shard_map/pallas_call | solution.py:24
  101.8 9.3 %all-to-all-done.4.got = s32[4,272,128]{2,1,0:T(8,128)S(1)} async-done(((s32[4,272,128]{2,1,0:T(8,128)}), s32[4,272,128]{2,1,0:T(8,128)S(1)}, u32[]{:S(2)}, u32[]{:S(2)}) %all-to-all-start.4) | async-done | bytes 557088 | tf_op jit(solution)/shard_map/all_to_all | solution.py:418
  111.1 1.1 shard_map.82
  (2 shorter events, 0.0 us)
Async XLA Ops:
  0.0 6.3 %copy-start.1 = (bf16[1,128,2048]{2,1,0:T(8,128)(2,1)S(1)}, bf16[1,128,2048]{2,1,0:T(8,128)(2,1)}, u32[]{:S(2)}) copy-start(bf16[1,128,2048]{2,1,0:T(8,128)(2,1)} %param.8) | copy-start | bytes 1572868
  0.0 6.3 %copy-start = (bf16[1,128,5120]{2,1,0:T(8,128)(2,1)S(1)}, bf16[1,128,5120]{2,1,0:T(8,128)(2,1)}, u32[]{:S(2)}) copy-start(bf16[1,128,5120]{2,1,0:T(8,128)(2,1)} %param.7) | copy-start | bytes 3932164
  0.0 1.1 copy-start.2
  1.9 17.1 %copy-start.3 = (f32[1,128,64]{1,2,0:T(8,128)S(1)}, f32[1,128,64]{1,2,0:T(8,128)}, u32[]{:S(2)}) copy-start(f32[1,128,64]{1,2,0:T(8,128)} %param.12) | copy-start | bytes 98308
  1.9 17.1 %copy-start.4 = (f32[4,2048]{1,0:T(4,128)S(1)}, f32[4,2048]{1,0:T(4,128)}, u32[]{:S(2)}) copy-start(f32[4,2048]{1,0:T(4,128)} %taps.5) | copy-start | bytes 98308
  1.9 15.2 %all-to-all-start = ((bf16[4,640,128]{2,1,0:T(8,128)(2,1)}), bf16[4,640,128]{2,1,0:T(8,128)(2,1)S(1)}, u32[]{:S(2)}, u32[]{:S(2)}) async-start(bf16[4,640,128]{2,1,0:T(8,128)(2,1)} %shard_map.75), calls=%async_computation | async-start | bytes 1310720 | tf_op jit(solution)/shard_map/all_to_all | solution.py:425
  6.6 8.1 %collective-permute-start = (bf16[3,7168]{1,0:T(4,128)(2,1)S(1)}, bf16[3,7168]{1,0:T(4,128)(2,1)S(1)}, u32[]{:S(2)}, u32[]{:S(2)}) collective-permute-start(bf16[3,7168]{1,0:T(4,128)(2,1)S(1)} %shard_map.73), channel_id=1, source_target_pairs={{0,8},{8,16},{16,24},{24,32},{32,40},{40,48},{48,56},{56,64},{64,7... | collective-permute-start | bytes 129032 | tf_op jit(solution)/shard_map/ppermute | solution.py:435
  17.1 4.0 %collective-permute-start.1 = (bf16[4,640,128]{2,1,0:T(8,128)(2,1)S(1)}, bf16[4,640,128]{2,1,0:T(8,128)(2,1)S(1)}, u32[]{:S(2)}, u32[]{:S(2)}) collective-permute-start(bf16[4,640,128]{2,1,0:T(8,128)(2,1)S(1)} %all-to-all-done.w), channel_id=1, source_target_pairs={{0,1},{1,0},{2,3},{3,2},{4,5},{5,4},{6,7},{7,6},{8,9},{9,8},{10,11... | collective-permute-start | bytes 1966088 | tf_op jit(solution)/shard_map/ppermute | solution.py:458
  19.1 2.0 %copy-start.5 = (f32[4,128]{1,0:T(4,128)S(1)}, f32[4,128]{1,0:T(4,128)}, u32[]{:S(2)}) copy-start(f32[4,128]{1,0:T(4,128)} %taps.4) | copy-start | bytes 6148
  23.0 19.1 %all-to-all-start.1 = ((s32[4,272,128]{2,1,0:T(8,128)}), s32[4,272,128]{2,1,0:T(8,128)S(1)}, u32[]{:S(2)}, u32[]{:S(2)}) async-start(s32[4,272,128]{2,1,0:T(8,128)} %get-tuple-element.25), calls=%async_computation.1 | async-start | bytes 1114112 | tf_op jit(solution)/shard_map/all_to_all | solution.py:418
  96.3 14.8 %all-to-all-start.4 = ((s32[4,272,128]{2,1,0:T(8,128)}), s32[4,272,128]{2,1,0:T(8,128)S(1)}, u32[]{:S(2)}, u32[]{:S(2)}) async-start(s32[4,272,128]{2,1,0:T(8,128)} %shard_map.80), calls=%async_computation.4 | async-start | bytes 1114112 | tf_op jit(solution)/shard_map/all_to_all | solution.py:418

commit v4 on v3

--- a/solution.py
+++ b/solution.py
@@ -316,6 +316,11 @@
     sent[pl.ds(half, heads, stride=message), :] = pack(scale.astype(jnp.int32), code_logs(passed))
 
 
+def members_of(groups):
+    rows = groups // GROUP
+    return [row * GROUP + place for place in range(GROUP) for row in range(rows)]
+
+
 def scan_kernel(headdim, core, got, sent, held, tops, factors, decays):
     half = headdim // 2
     message = half + 1
@@ -324,14 +329,17 @@
     notes = got[pl.ds(half, groups, stride=message), :]
     factors[...] = down(high_of(notes).astype(jnp.float32))
     decays[...] = jnp.broadcast_to(jnp.exp(read_logs(notes)), decays.shape)
-    first = codes_of(got[(groups - 1) * message : (groups - 1) * message + half, :])
-    carried = first * factors[groups - 1 : groups, :] * jnp.where(core[0] > 0, 1.0, 0.0)
+    listed = members_of(groups)
+    last = listed.index(groups - 1)
+    opening = codes_of(got[last * message : last * message + half, :])
+    carried = opening * factors[last : last + 1, :] * jnp.where(core[0] > 0, 1.0, 0.0)
     for group in range(groups):
-        held[group * headdim : (group + 1) * headdim, :] = carried
-        tops[group : group + 1, :] = jnp.max(jnp.abs(carried), axis=0, keepdims=True)
-        state = codes_of(got[group * message : group * message + half, :])
-        state = state * factors[group : group + 1, :]
-        carried = decays[group : group + 1, :] * carried + state
+        slot = listed.index(group)
+        held[slot * headdim : (slot + 1) * headdim, :] = carried
+        tops[slot : slot + 1, :] = jnp.max(jnp.abs(carried), axis=0, keepdims=True)
+        state = codes_of(got[slot * message : slot * message + half, :])
+        state = state * factors[slot : slot + 1, :]
+        carried = decays[slot : slot + 1, :] * carried + state
     scale = scale_codes(tops[...])
     sent[pl.ds(half, groups, stride=message), :] = lax.shift_left(scale.astype(jnp.int32), 16)
     factors[...] = up(scale)
@@ -405,7 +413,7 @@
         for group in range(group_count)
     ]
     far = [
-        [device(side, part, group * GROUP + i) for group in range(group_count)]
+        [device(side, part, group * GROUP + i) for group in members_of(group_count)]
         for side, part in sides
         for i in range(GROUP)
     ]
@@ -454,7 +462,7 @@
         scratch=scratch,
     )
 
-    w_own, before = lax.optimization_barrier((w_own, before))
+    w_own, before, core, wraps = lax.optimization_barrier((w_own, before, core, wraps))
     w_other = lax.ppermute(w_own, "fsdp", [(i, i ^ 1) for i in range(parts)])
     begun, rest = call(
         partial_kernel,

time: 113 us -> 111 us (0.982)
  blocking collectives: 52.6 us -> 71.5 us
  waiting for transfers between devices: 29.2 us -> 15.1 us
  starting transfers between devices: 19.5 us -> 13.5 us
    all_to_all x2 -> x3, blocking collectives: 52.6 us -> 71.5 us  [exchange(): lax.all_to_all(sent, ('seq', 'fsdp'), 0, 0, axis_index_groups=members)]
    all_to_all x2 -> x1, waiting for transfers between devices: 22.4 us -> 8.31 us  [exchange(): lax.all_to_all(sent, ('seq', 'fsdp'), 0, 0, axis_index_groups=members)]
    all_to_all x2 -> x1, starting transfers between devices: 9.48 us -> 3.48 us  [exchange(): lax.all_to_all(sent, ('seq', 'fsdp'), 0, 0, axis_index_groups=members)]
  transfers between devices with their start and end apart: 5 -> 4, of which waited for: 5 -> 4; matrix products, arithmetic and copies ran while one was open for 0% -> 0% of each run, Pallas kernels for 3% -> 3%
where the time goes in v4:
time: 111 us; the launch traced here: 110 us
  blocking collectives  71.5 us (64%)
  waiting for transfers between devices  15.1 us (14%)
  starting transfers between devices  13.5 us (12%)
  Pallas kernels  8.2 us (7%)
    all_to_all x3, blocking collectives, exchange(): lax.all_to_all(sent, ('seq', 'fsdp'), 0, 0, axis_index_groups=members)  71.5 us
    all_to_all x1, waiting for transfers between devices, exchange(): lax.all_to_all(sent, ('seq', 'fsdp'), 0, 0, axis_index_groups=members)  8.31 us
    pallas_call x9, Pallas kernels, call(): pl.pallas_call(kernel, in_specs=[pl.BlockSpec(memory_space=place) for pla...  7.33 us
    all_to_all x1, starting transfers between devices, on_device(): w_own = lax.all_to_all(w_copies, 'fsdp', 0, 0, axis_index_groups=chips)  4.3 us
    ppermute x1, waiting for transfers between devices, on_device(): before = lax.ppermute(edge, 'seq', [(i, i + 1) for i in range(shards - 1)])  4.25 us
    ppermute x1, starting transfers between devices, on_device(): before = lax.ppermute(edge, 'seq', [(i, i + 1) for i in range(shards - 1)])  3.83 us
    all_to_all x1, starting transfers between devices, exchange(): lax.all_to_all(sent, ('seq', 'fsdp'), 0, 0, axis_index_groups=members)  3.48 us
    all_to_all x1, waiting for transfers between devices, on_device(): w_own = lax.all_to_all(w_copies, 'fsdp', 0, 0, axis_index_groups=chips)  2.38 us
  transfers between devices with their start and end apart: 4, of which 4 were waited for; matrix products, arithmetic and copies ran while one was open for 0% of the time, Pallas kernels for 3%

profile of v4, /device:TPU:32, one launch (start us, length us, event | category | flops | bytes accessed | tf_op | source)
XLA Modules:
  0.0 110.1 jit_solution(3355751977187878152)
XLA Ops:
  0.0 0.0 copy-start
  0.0 0.0 copy-start.2
  0.0 1.0 copy-done.2
  1.1 0.9 shard_map.73
  1.9 4.3 %all-to-all-start = ((bf16[4,640,128]{2,1,0:T(8,128)(2,1)}), bf16[4,640,128]{2,1,0:T(8,128)(2,1)S(1)}, u32[]{:S(2)}, u32[]{:S(2)}) async-start(bf16[4,640,128]{2,1,0:T(8,128)(2,1)} %shard_map.73), calls=%async_computation | async-start | bytes 1310720 | tf_op jit(solution)/shard_map/all_to_all | solution.py:433
  6.2 0.0 copy-start.3
  6.2 0.0 copy-start.4
  6.2 0.0 copy-done.1
  6.2 0.0 copy-done
  6.2 0.3 shard_map.74
  6.6 3.8 %collective-permute-start = (bf16[3,7168]{1,0:T(4,128)(2,1)S(1)}, bf16[3,7168]{1,0:T(4,128)(2,1)S(1)}, u32[]{:S(2)}, u32[]{:S(2)}) collective-permute-start(bf16[3,7168]{1,0:T(4,128)(2,1)S(1)} %shard_map.74), channel_id=1, source_target_pairs={{0,8},{8,16},{16,24},{24,32},{32,40},{40,48},{48,56},{56,64},{64,7... | collective-permute-start | bytes 129032 | tf_op jit(solution)/shard_map/ppermute | solution.py:443
  10.5 4.3 %collective-permute-done.before = bf16[3,7168]{1,0:T(4,128)(2,1)S(1)} collective-permute-done((bf16[3,7168]{1,0:T(4,128)(2,1)S(1)}, bf16[3,7168]{1,0:T(4,128)(2,1)S(1)}, u32[]{:S(2)}, u32[]{:S(2)}) %collective-permute-start) | collective-permute-done | bytes 43040 | tf_op jit(solution)/shard_map/ppermute | solution.py:443
  14.7 2.4 %all-to-all-done.w = bf16[4,640,128]{2,1,0:T(8,128)(2,1)S(1)} async-done(((bf16[4,640,128]{2,1,0:T(8,128)(2,1)}), bf16[4,640,128]{2,1,0:T(8,128)(2,1)S(1)}, u32[]{:S(2)}, u32[]{:S(2)}) %all-to-all-start) | async-done | bytes 655392 | tf_op jit(solution)/shard_map/all_to_all | solution.py:433
  17.1 1.9 %collective-permute-start.1 = (bf16[4,640,128]{2,1,0:T(8,128)(2,1)S(1)}, bf16[4,640,128]{2,1,0:T(8,128)(2,1)S(1)}, u32[]{:S(2)}, u32[]{:S(2)}) collective-permute-start(bf16[4,640,128]{2,1,0:T(8,128)(2,1)S(1)} %all-to-all-done.w), channel_id=1, source_target_pairs={{0,1},{1,0},{2,3},{3,2},{4,5},{5,4},{6,7},{7,6},{8,9},{9,8},{10,11... | collective-permute-start | bytes 1966088 | tf_op jit(solution)/shard_map/ppermute | solution.py:466
  19.0 0.0 copy-done.3
  19.0 0.0 copy-done.4
  19.0 0.0 copy-start.5
  19.1 1.2 %shard_map.75 = (bf16[2048,256]{1,0:T(8,128)(2,1)S(1)}, f32[64,128]{1,0:T(8,128)S(1)}, bf16[16,5120]{1,0:T(8,128)(2,1)S(1)}) custom-call(f32[64,128]{1,0:T(8,128)S(1)} %bitcast.23, bf16[128,2048]{1,0:T(8,128)(2,1)S(1)} %bitcast.17, bf16[3,7168]{1,0:T(4,128)(2,1)S(1)} %collective-permute-done.before, f32[4,2048]{1,0:T(4,128)S(1)} %copy-done.4), custom_call_target="tpu_custom_call" | custom-call | tf_op jit(solution)/shard_map/pallas_call | solution.py:24
  20.2 0.7 shard_map.76
  21.0 0.1 collective-permute-done.1.w
  21.1 0.0 copy-done.5
  21.1 1.0 shard_map.77
  22.1 18.1 %all_to_all.25.got = s32[4,272,128]{2,1,0:T(8,128)S(1)} all-to-all(s32[4,272,128]{2,1,0:T(8,128)S(1)} %get-tuple-element.29), channel_id=1, replica_groups={{0,8,16,24},{32,40,48,56},{64,72,80,88},{96,104,112,120},{128,136,144,1..., dimensions={0} | all-to-all | bytes 1114112 | tf_op jit(solution)/shard_map/all_to_all | solution.py:426
  40.2 0.3 shard_map.78
  40.6 31.8 %all_to_all.26 = s32[16,1,2176]{2,1,0:T(1,128)S(1)} all-to-all(s32[16,1,2176]{2,1,0:T(1,128)S(1)} %bitcast.22), channel_id=1, replica_groups={{0,128,256,384,32,160,288,416,64,192,320,448,96,224,352,480},{8,136,264..., dimensions={0} | all-to-all | bytes 278528 | tf_op jit(solution)/shard_map/all_to_all | solution.py:426
  72.4 0.2 shard_map.79
  72.6 21.6 %all_to_all.27 = s32[16,1,2176]{2,1,0:T(1,128)S(1)} all-to-all(s32[16,1,2176]{2,1,0:T(1,128)S(1)} %bitcast.21), channel_id=1, replica_groups={{0,128,256,384,32,160,288,416,64,192,320,448,96,224,352,480},{8,136,264..., dimensions={0} | all-to-all | bytes 278528 | tf_op jit(solution)/shard_map/all_to_all | solution.py:426
  94.1 1.2 %shard_map.80 = s32[4,272,128]{2,1,0:T(8,128)} custom-call(s32[272,128]{1,0:T(8,128)S(1)} %bitcast.19, f32[4,512,128]{2,1,0:T(8,128)S(1)} %get-tuple-element.31.prefix, f32[4,16,128]{2,1,0:T(8,128)S(1)} %get-tuple-element.32.decay), custom_call_target="tpu_custom_call" | custom-call | tf_op jit(solution)/shard_map/pallas_call | solution.py:24
  95.3 3.5 %all-to-all-start.4 = ((s32[4,272,128]{2,1,0:T(8,128)}), s32[4,272,128]{2,1,0:T(8,128)S(1)}, u32[]{:S(2)}, u32[]{:S(2)}) async-start(s32[4,272,128]{2,1,0:T(8,128)} %shard_map.80), calls=%async_computation.4 | async-start | bytes 1114112 | tf_op jit(solution)/shard_map/all_to_all | solution.py:426
  99.4 1.3 %shard_map.81 = (f32[2048,128]{1,0:T(8,128)S(1)}, f32[64,128]{1,0:T(8,128)S(1)}) custom-call(s32[1]{0:T(128)} %bitcast.13.accepted, f32[64,128]{1,0:T(8,128)S(1)} %bitcast.24, bf16[128,2048]{1,0:T(8,128)(2,1)S(1)} %bitcast.18, bf16[3,7168]{1,0:T(4,128)(2,1)S(1)} %collective-permute-done.before, f32[4,2048]{1,0:T(4,128)S(1)} %copy-done.4, ...), custom_call_target="tpu_custom_call" | custom-call | tf_op jit(solution)/shard_map/pallas_call | solution.py:24
  100.8 8.3 %all-to-all-done.4.got = s32[4,272,128]{2,1,0:T(8,128)S(1)} async-done(((s32[4,272,128]{2,1,0:T(8,128)}), s32[4,272,128]{2,1,0:T(8,128)S(1)}, u32[]{:S(2)}, u32[]{:S(2)}) %all-to-all-start.4) | async-done | bytes 557088 | tf_op jit(solution)/shard_map/all_to_all | solution.py:426
  109.1 1.1 shard_map.82
  (1 shorter events, 0.0 us)
Async XLA Ops:
  0.0 6.2 %copy-start.1 = (bf16[1,128,2048]{2,1,0:T(8,128)(2,1)S(1)}, bf16[1,128,2048]{2,1,0:T(8,128)(2,1)}, u32[]{:S(2)}) copy-start(bf16[1,128,2048]{2,1,0:T(8,128)(2,1)} %param.8) | copy-start | bytes 1572868
  0.0 6.2 %copy-start = (bf16[1,128,5120]{2,1,0:T(8,128)(2,1)S(1)}, bf16[1,128,5120]{2,1,0:T(8,128)(2,1)}, u32[]{:S(2)}) copy-start(bf16[1,128,5120]{2,1,0:T(8,128)(2,1)} %param.7) | copy-start | bytes 3932164
  0.0 1.1 copy-start.2
  1.9 15.2 %all-to-all-start = ((bf16[4,640,128]{2,1,0:T(8,128)(2,1)}), bf16[4,640,128]{2,1,0:T(8,128)(2,1)S(1)}, u32[]{:S(2)}, u32[]{:S(2)}) async-start(bf16[4,640,128]{2,1,0:T(8,128)(2,1)} %shard_map.73), calls=%async_computation | async-start | bytes 1310720 | tf_op jit(solution)/shard_map/all_to_all | solution.py:433
  6.2 12.8 %copy-start.3 = (f32[1,128,64]{1,2,0:T(8,128)S(1)}, f32[1,128,64]{1,2,0:T(8,128)}, u32[]{:S(2)}) copy-start(f32[1,128,64]{1,2,0:T(8,128)} %param.12) | copy-start | bytes 98308
  6.2 12.8 %copy-start.4 = (f32[4,2048]{1,0:T(4,128)S(1)}, f32[4,2048]{1,0:T(4,128)}, u32[]{:S(2)}) copy-start(f32[4,2048]{1,0:T(4,128)} %taps.5) | copy-start | bytes 98308
  6.6 8.1 %collective-permute-start = (bf16[3,7168]{1,0:T(4,128)(2,1)S(1)}, bf16[3,7168]{1,0:T(4,128)(2,1)S(1)}, u32[]{:S(2)}, u32[]{:S(2)}) collective-permute-start(bf16[3,7168]{1,0:T(4,128)(2,1)S(1)} %shard_map.74), channel_id=1, source_target_pairs={{0,8},{8,16},{16,24},{24,32},{32,40},{40,48},{48,56},{56,64},{64,7... | collective-permute-start | bytes 129032 | tf_op jit(solution)/shard_map/ppermute | solution.py:443
  17.1 4.0 %collective-permute-start.1 = (bf16[4,640,128]{2,1,0:T(8,128)(2,1)S(1)}, bf16[4,640,128]{2,1,0:T(8,128)(2,1)S(1)}, u32[]{:S(2)}, u32[]{:S(2)}) collective-permute-start(bf16[4,640,128]{2,1,0:T(8,128)(2,1)S(1)} %all-to-all-done.w), channel_id=1, source_target_pairs={{0,1},{1,0},{2,3},{3,2},{4,5},{5,4},{6,7},{7,6},{8,9},{9,8},{10,11... | collective-permute-start | bytes 1966088 | tf_op jit(solution)/shard_map/ppermute | solution.py:466
  19.0 2.0 %copy-start.5 = (f32[4,128]{1,0:T(4,128)S(1)}, f32[4,128]{1,0:T(4,128)}, u32[]{:S(2)}) copy-start(f32[4,128]{1,0:T(4,128)} %taps.4) | copy-start | bytes 6148
  95.3 13.8 %all-to-all-start.4 = ((s32[4,272,128]{2,1,0:T(8,128)}), s32[4,272,128]{2,1,0:T(8,128)S(1)}, u32[]{:S(2)}, u32[]{:S(2)}) async-start(s32[4,272,128]{2,1,0:T(8,128)} %shard_map.80), calls=%async_computation.4 | async-start | bytes 1114112 | tf_op jit(solution)/shard_map/all_to_all | solution.py:426

commit v5 on v4

--- a/solution.py
+++ b/solution.py
@@ -318,7 +318,8 @@
 
 def members_of(groups):
     rows = groups // GROUP
-    return [row * GROUP + place for place in range(GROUP) for row in range(rows)]
+    places = [(place + GROUP // 2) % GROUP for place in range(GROUP)]
+    return [row * GROUP + place for place in places for row in reversed(range(rows))]
 
 
 def scan_kernel(headdim, core, got, sent, held, tops, factors, decays):

time: 111 us -> 106 us (0.955)
  the two profiles are of different devices: /device:TPU:32 before, /device:TPU:1 now
where the time goes in v5:
time: 106 us; the launch traced here: 105 us
  blocking collectives  58.3 us (55%)
  starting transfers between devices  26.8 us (25%)
  waiting for transfers between devices  9.99 us (9%)
  Pallas kernels  8.19 us (8%)
  local copies, waits for them, and re-layouts  1.07 us (1%)
    all_to_all x3, blocking collectives, exchange(): lax.all_to_all(sent, ('seq', 'fsdp'), 0, 0, axis_index_groups=members)  58.3 us
    all_to_all x1, starting transfers between devices, exchange(): lax.all_to_all(sent, ('seq', 'fsdp'), 0, 0, axis_index_groups=members)  9.85 us
    ppermute x1, starting transfers between devices, on_device(): w_other = lax.ppermute(w_own, 'fsdp', [(i, i ^ 1) for i in range(parts)])  8.54 us
    pallas_call x9, Pallas kernels, call(): pl.pallas_call(kernel, in_specs=[pl.BlockSpec(memory_space=place) for pla...  7.33 us
    all_to_all x1, waiting for transfers between devices, exchange(): lax.all_to_all(sent, ('seq', 'fsdp'), 0, 0, axis_index_groups=members)  6.32 us
    all_to_all x1, starting transfers between devices, on_device(): w_own = lax.all_to_all(w_copies, 'fsdp', 0, 0, axis_index_groups=chips)  4.85 us
    ppermute x1, starting transfers between devices, on_device(): before = lax.ppermute(edge, 'seq', [(i, i + 1) for i in range(shards - 1)])  3.54 us
    all_to_all x1, waiting for transfers between devices, on_device(): w_own = lax.all_to_all(w_copies, 'fsdp', 0, 0, axis_index_groups=chips)  2.48 us
  transfers between devices with their start and end apart: 4, of which 3 were waited for; matrix products, arithmetic and copies ran while one was open for 0% of the time, Pallas kernels for 3%

profile of v5, /device:TPU:1, one launch (start us, length us, event | category | flops | bytes accessed | tf_op | source)
XLA Modules:
  0.0 105.1 jit_solution(14144770748710097402)
XLA Ops:
  0.0 0.0 copy-start.1
  0.0 0.0 copy-start
  0.0 1.0 copy-done.2
  1.1 0.9 shard_map.73
  1.9 4.9 %all-to-all-start = ((bf16[4,640,128]{2,1,0:T(8,128)(2,1)}), bf16[4,640,128]{2,1,0:T(8,128)(2,1)S(1)}, u32[]{:S(2)}, u32[]{:S(2)}) async-start(bf16[4,640,128]{2,1,0:T(8,128)(2,1)} %shard_map.73), calls=%async_computation | async-start | bytes 1310720 | tf_op jit(solution)/shard_map/all_to_all | solution.py:434
  6.8 0.0 copy-start.3
  6.8 0.0 copy-start.4
  6.8 0.0 copy-done.1
  6.8 0.0 copy-done
  6.8 0.3 shard_map.74
  7.1 3.5 %collective-permute-start = (bf16[3,7168]{1,0:T(4,128)(2,1)S(1)}, bf16[3,7168]{1,0:T(4,128)(2,1)S(1)}, u32[]{:S(2)}, u32[]{:S(2)}) collective-permute-start(bf16[3,7168]{1,0:T(4,128)(2,1)S(1)} %shard_map.74), channel_id=1, source_target_pairs={{0,8},{8,16},{16,24},{24,32},{32,40},{40,48},{48,56},{56,64},{64,7... | collective-permute-start | bytes 129032 | tf_op jit(solution)/shard_map/ppermute | solution.py:444
  10.8 1.2 %collective-permute-done.before = bf16[3,7168]{1,0:T(4,128)(2,1)S(1)} collective-permute-done((bf16[3,7168]{1,0:T(4,128)(2,1)S(1)}, bf16[3,7168]{1,0:T(4,128)(2,1)S(1)}, u32[]{:S(2)}, u32[]{:S(2)}) %collective-permute-start) | collective-permute-done | bytes 43040 | tf_op jit(solution)/shard_map/ppermute | solution.py:444
  11.9 2.5 %all-to-all-done.w = bf16[4,640,128]{2,1,0:T(8,128)(2,1)S(1)} async-done(((bf16[4,640,128]{2,1,0:T(8,128)(2,1)}), bf16[4,640,128]{2,1,0:T(8,128)(2,1)S(1)}, u32[]{:S(2)}, u32[]{:S(2)}) %all-to-all-start) | async-done | bytes 655392 | tf_op jit(solution)/shard_map/all_to_all | solution.py:434
  14.4 8.5 %collective-permute-start.1 = (bf16[4,640,128]{2,1,0:T(8,128)(2,1)S(1)}, bf16[4,640,128]{2,1,0:T(8,128)(2,1)S(1)}, u32[]{:S(2)}, u32[]{:S(2)}) collective-permute-start(bf16[4,640,128]{2,1,0:T(8,128)(2,1)S(1)} %all-to-all-done.w), channel_id=1, source_target_pairs={{0,1},{1,0},{2,3},{3,2},{4,5},{5,4},{6,7},{7,6},{8,9},{9,8},{10,11... | collective-permute-start | bytes 1966088 | tf_op jit(solution)/shard_map/ppermute | solution.py:467
  23.0 0.0 copy-done.3
  23.0 0.0 copy-done.4
  23.0 0.0 copy-start.5
  23.0 1.2 %shard_map.75 = (bf16[2048,256]{1,0:T(8,128)(2,1)S(1)}, f32[64,128]{1,0:T(8,128)S(1)}, bf16[16,5120]{1,0:T(8,128)(2,1)S(1)}) custom-call(f32[64,128]{1,0:T(8,128)S(1)} %bitcast.23, bf16[128,2048]{1,0:T(8,128)(2,1)S(1)} %bitcast.17, bf16[3,7168]{1,0:T(4,128)(2,1)S(1)} %collective-permute-done.before, f32[4,2048]{1,0:T(4,128)S(1)} %copy-done.4), custom_call_target="tpu_custom_call" | custom-call | tf_op jit(solution)/shard_map/pallas_call | solution.py:24
  24.2 0.7 shard_map.76
  24.9 0.0 collective-permute-done.1.w
  24.9 0.0 copy-done.5
  24.9 1.0 shard_map.77
  25.9 21.7 %all_to_all.25.got = s32[4,272,128]{2,1,0:T(8,128)S(1)} all-to-all(s32[4,272,128]{2,1,0:T(8,128)S(1)} %get-tuple-element.29), channel_id=1, replica_groups={{0,8,16,24},{32,40,48,56},{64,72,80,88},{96,104,112,120},{128,136,144,1..., dimensions={0} | all-to-all | bytes 1114112 | tf_op jit(solution)/shard_map/all_to_all | solution.py:427
  47.7 0.3 shard_map.78
  48.0 19.5 %all_to_all.26 = s32[16,1,2176]{2,1,0:T(1,128)S(1)} all-to-all(s32[16,1,2176]{2,1,0:T(1,128)S(1)} %bitcast.22), channel_id=1, replica_groups={{448,320,192,64,480,352,224,96,384,256,128,0,416,288,160,32},{456,328,2..., dimensions={0} | all-to-all | bytes 278528 | tf_op jit(solution)/shard_map/all_to_all | solution.py:427
  67.5 0.2 shard_map.79
  67.7 17.1 %all_to_all.27 = s32[16,1,2176]{2,1,0:T(1,128)S(1)} all-to-all(s32[16,1,2176]{2,1,0:T(1,128)S(1)} %bitcast.21), channel_id=1, replica_groups={{448,320,192,64,480,352,224,96,384,256,128,0,416,288,160,32},{456,328,2..., dimensions={0} | all-to-all | bytes 278528 | tf_op jit(solution)/shard_map/all_to_all | solution.py:427
  84.8 1.2 %shard_map.80 = s32[4,272,128]{2,1,0:T(8,128)} custom-call(s32[272,128]{1,0:T(8,128)S(1)} %bitcast.19, f32[4,512,128]{2,1,0:T(8,128)S(1)} %get-tuple-element.31.prefix, f32[4,16,128]{2,1,0:T(8,128)S(1)} %get-tuple-element.32.decay), custom_call_target="tpu_custom_call" | custom-call | tf_op jit(solution)/shard_map/pallas_call | solution.py:24
  85.9 9.9 %all-to-all-start.4 = ((s32[4,272,128]{2,1,0:T(8,128)}), s32[4,272,128]{2,1,0:T(8,128)S(1)}, u32[]{:S(2)}, u32[]{:S(2)}) async-start(s32[4,272,128]{2,1,0:T(8,128)} %shard_map.80), calls=%async_computation.4 | async-start | bytes 1114112 | tf_op jit(solution)/shard_map/all_to_all | solution.py:427
  96.4 1.3 %shard_map.81 = (f32[2048,128]{1,0:T(8,128)S(1)}, f32[64,128]{1,0:T(8,128)S(1)}) custom-call(s32[1]{0:T(128)} %bitcast.13.accepted, f32[64,128]{1,0:T(8,128)S(1)} %bitcast.24, bf16[128,2048]{1,0:T(8,128)(2,1)S(1)} %bitcast.18, bf16[3,7168]{1,0:T(4,128)(2,1)S(1)} %collective-permute-done.before, f32[4,2048]{1,0:T(4,128)S(1)} %copy-done.4, ...), custom_call_target="tpu_custom_call" | custom-call | tf_op jit(solution)/shard_map/pallas_call | solution.py:24
  97.8 6.3 %all-to-all-done.4.got = s32[4,272,128]{2,1,0:T(8,128)S(1)} async-done(((s32[4,272,128]{2,1,0:T(8,128)}), s32[4,272,128]{2,1,0:T(8,128)S(1)}, u32[]{:S(2)}, u32[]{:S(2)}) %all-to-all-start.4) | async-done | bytes 557088 | tf_op jit(solution)/shard_map/all_to_all | solution.py:427
  104.1 1.1 %shard_map.82 = f32[2048,128]{1,0:T(8,128)} custom-call(s32[4,272,128]{2,1,0:T(8,128)S(1)} %all-to-all-done.4.got, f32[64,128]{1,0:T(8,128)S(1)} %get-tuple-element.35.kept, f32[2048,128]{1,0:T(8,128)S(1)} %get-tuple-element.36.part), custom_call_target="tpu_custom_call" | custom-call | tf_op jit(solution)/shard_map/pallas_call | solution.py:24
  (1 shorter events, 0.0 us)
Async XLA Ops:
  0.0 6.8 %copy-start.1 = (bf16[1,128,2048]{2,1,0:T(8,128)(2,1)S(1)}, bf16[1,128,2048]{2,1,0:T(8,128)(2,1)}, u32[]{:S(2)}) copy-start(bf16[1,128,2048]{2,1,0:T(8,128)(2,1)} %param.8) | copy-start | bytes 1572868
  0.0 6.8 %copy-start = (bf16[1,128,5120]{2,1,0:T(8,128)(2,1)S(1)}, bf16[1,128,5120]{2,1,0:T(8,128)(2,1)}, u32[]{:S(2)}) copy-start(bf16[1,128,5120]{2,1,0:T(8,128)(2,1)} %param.7) | copy-start | bytes 3932164
  0.0 1.1 copy-start.2
  1.9 12.5 %all-to-all-start = ((bf16[4,640,128]{2,1,0:T(8,128)(2,1)}), bf16[4,640,128]{2,1,0:T(8,128)(2,1)S(1)}, u32[]{:S(2)}, u32[]{:S(2)}) async-start(bf16[4,640,128]{2,1,0:T(8,128)(2,1)} %shard_map.73), calls=%async_computation | async-start | bytes 1310720 | tf_op jit(solution)/shard_map/all_to_all | solution.py:434
  6.8 16.2 %copy-start.3 = (f32[1,128,64]{1,2,0:T(8,128)S(1)}, f32[1,128,64]{1,2,0:T(8,128)}, u32[]{:S(2)}) copy-start(f32[1,128,64]{1,2,0:T(8,128)} %param.12) | copy-start | bytes 98308
  6.8 16.2 %copy-start.4 = (f32[4,2048]{1,0:T(4,128)S(1)}, f32[4,2048]{1,0:T(4,128)}, u32[]{:S(2)}) copy-start(f32[4,2048]{1,0:T(4,128)} %taps.5) | copy-start | bytes 98308
  7.1 4.8 %collective-permute-start = (bf16[3,7168]{1,0:T(4,128)(2,1)S(1)}, bf16[3,7168]{1,0:T(4,128)(2,1)S(1)}, u32[]{:S(2)}, u32[]{:S(2)}) collective-permute-start(bf16[3,7168]{1,0:T(4,128)(2,1)S(1)} %shard_map.74), channel_id=1, source_target_pairs={{0,8},{8,16},{16,24},{24,32},{32,40},{40,48},{48,56},{56,64},{64,7... | collective-permute-start | bytes 129032 | tf_op jit(solution)/shard_map/ppermute | solution.py:444
  14.4 10.5 %collective-permute-start.1 = (bf16[4,640,128]{2,1,0:T(8,128)(2,1)S(1)}, bf16[4,640,128]{2,1,0:T(8,128)(2,1)S(1)}, u32[]{:S(2)}, u32[]{:S(2)}) collective-permute-start(bf16[4,640,128]{2,1,0:T(8,128)(2,1)S(1)} %all-to-all-done.w), channel_id=1, source_target_pairs={{0,1},{1,0},{2,3},{3,2},{4,5},{5,4},{6,7},{7,6},{8,9},{9,8},{10,11... | collective-permute-start | bytes 1966088 | tf_op jit(solution)/shard_map/ppermute | solution.py:467
  23.0 1.9 %copy-start.5 = (f32[4,128]{1,0:T(4,128)S(1)}, f32[4,128]{1,0:T(4,128)}, u32[]{:S(2)}) copy-start(f32[4,128]{1,0:T(4,128)} %taps.4) | copy-start | bytes 6148
  85.9 18.2 %all-to-all-start.4 = ((s32[4,272,128]{2,1,0:T(8,128)}), s32[4,272,128]{2,1,0:T(8,128)S(1)}, u32[]{:S(2)}, u32[]{:S(2)}) async-start(s32[4,272,128]{2,1,0:T(8,128)} %shard_map.80), calls=%async_computation.4 | async-start | bytes 1114112 | tf_op jit(solution)/shard_map/all_to_all | solution.py:427

commit v6 on v5

--- a/solution.py
+++ b/solution.py
@@ -312,8 +312,8 @@
     scale = scale_codes(jnp.max(jnp.abs(carried), axis=1))
     words = words_of(carried * up(scale)[:, None, :])
     for head in range(heads):
-        sent[head * message : head * message + half, :] = words[head]
-    sent[pl.ds(half, heads, stride=message), :] = pack(scale.astype(jnp.int32), code_logs(passed))
+        sent[head * message + 1 : (head + 1) * message, :] = words[head]
+    sent[pl.ds(0, heads, stride=message), :] = pack(scale.astype(jnp.int32), code_logs(passed))
 
 
 def members_of(groups):
@@ -327,26 +327,26 @@
     message = half + 1
     groups = got.shape[0] // message
     size = got.shape[1]
-    notes = got[pl.ds(half, groups, stride=message), :]
+    notes = got[pl.ds(0, groups, stride=message), :]
     factors[...] = down(high_of(notes).astype(jnp.float32))
     decays[...] = jnp.broadcast_to(jnp.exp(read_logs(notes)), decays.shape)
     listed = members_of(groups)
     last = listed.index(groups - 1)
-    opening = codes_of(got[last * message : last * message + half, :])
+    opening = codes_of(got[last * message + 1 : (last + 1) * message, :])
     carried = opening * factors[last : last + 1, :] * jnp.where(core[0] > 0, 1.0, 0.0)
     for group in range(groups):
         slot = listed.index(group)
         held[slot * headdim : (slot + 1) * headdim, :] = carried
         tops[slot : slot + 1, :] = jnp.max(jnp.abs(carried), axis=0, keepdims=True)
-        state = codes_of(got[slot * message : slot * message + half, :])
+        state = codes_of(got[slot * message + 1 : (slot + 1) * message, :])
         state = state * factors[slot : slot + 1, :]
         carried = decays[slot : slot + 1, :] * carried + state
     scale = scale_codes(tops[...])
-    sent[pl.ds(half, groups, stride=message), :] = lax.shift_left(scale.astype(jnp.int32), 16)
+    sent[pl.ds(0, groups, stride=message), :] = lax.shift_left(scale.astype(jnp.int32), 16)
     factors[...] = up(scale)
     for group in range(groups):
         scaled = held[group * headdim : (group + 1) * headdim, :] * factors[group : group + 1, :]
-        sent[group * message : group * message + half, :] = words_of(scaled)
+        sent[group * message + 1 : (group + 1) * message, :] = words_of(scaled)
 
 
 def incoming_kernel(headdim, got, prefix, decay, sent, held, factors, staged, arrived):
@@ -354,10 +354,10 @@
     heads = rows // headdim
     half = headdim // 2
     message = half + 1
-    notes = got[pl.ds(half, heads, stride=message), :]
+    notes = got[pl.ds(0, heads, stride=message), :]
     factors[...] = down(high_of(notes).astype(jnp.float32))
     for head in range(heads):
-        state = codes_of(got[head * message : head * message + half, :])
+        state = codes_of(got[head * message + 1 : (head + 1) * message, :])
         held[head] = state * factors[head : head + 1, :]
     for shard in range(shards):
         local = prefix[shard].reshape(heads, headdim, size)

time: 106 us -> 106 us (level)
  no operation moved by 1% of the time
where the time goes in v6:
time: 106 us; the launch traced here: 105 us
  blocking collectives  58.3 us (55%)
  starting transfers between devices  26.8 us (25%)
  waiting for transfers between devices  9.99 us (9%)
  Pallas kernels  8.19 us (8%)
  local copies, waits for them, and re-layouts  1.07 us (1%)
    all_to_all x3, blocking collectives, exchange(): lax.all_to_all(sent, ('seq', 'fsdp'), 0, 0, axis_index_groups=members)  58.3 us
    all_to_all x1, starting transfers between devices, exchange(): lax.all_to_all(sent, ('seq', 'fsdp'), 0, 0, axis_index_groups=members)  9.85 us
    ppermute x1, starting transfers between devices, on_device(): w_other = lax.ppermute(w_own, 'fsdp', [(i, i ^ 1) for i in range(parts)])  8.54 us
    pallas_call x9, Pallas kernels, call(): pl.pallas_call(kernel, in_specs=[pl.BlockSpec(memory_space=place) for pla...  7.33 us
    all_to_all x1, waiting for transfers between devices, exchange(): lax.all_to_all(sent, ('seq', 'fsdp'), 0, 0, axis_index_groups=members)  6.32 us
    all_to_all x1, starting transfers between devices, on_device(): w_own = lax.all_to_all(w_copies, 'fsdp', 0, 0, axis_index_groups=chips)  4.85 us
    ppermute x1, starting transfers between devices, on_device(): before = lax.ppermute(edge, 'seq', [(i, i + 1) for i in range(shards - 1)])  3.54 us
    all_to_all x1, waiting for transfers between devices, on_device(): w_own = lax.all_to_all(w_copies, 'fsdp', 0, 0, axis_index_groups=chips)  2.48 us
  transfers between devices with their start and end apart: 4, of which 3 were waited for; matrix products, arithmetic and copies ran while one was open for 0% of the time, Pallas kernels for 3%

profile of v6, /device:TPU:1, one launch (start us, length us, event | category | flops | bytes accessed | tf_op | source)
XLA Modules:
  0.0 105.1 jit_solution(13655140570519822778)
XLA Ops:
  0.0 0.0 copy-start.1
  0.0 0.0 copy-start
  0.0 0.0 copy-start.2
  0.0 1.0 copy-done.2
  1.1 0.9 shard_map.73
  1.9 4.9 %all-to-all-start = ((bf16[4,640,128]{2,1,0:T(8,128)(2,1)}), bf16[4,640,128]{2,1,0:T(8,128)(2,1)S(1)}, u32[]{:S(2)}, u32[]{:S(2)}) async-start(bf16[4,640,128]{2,1,0:T(8,128)(2,1)} %shard_map.73), calls=%async_computation | async-start | bytes 1310720 | tf_op jit(solution)/shard_map/all_to_all | solution.py:434
  6.8 0.0 copy-start.3
  6.8 0.0 copy-done.1
  6.8 0.0 copy-done
  6.8 0.3 shard_map.74
  7.1 3.5 %collective-permute-start = (bf16[3,7168]{1,0:T(4,128)(2,1)S(1)}, bf16[3,7168]{1,0:T(4,128)(2,1)S(1)}, u32[]{:S(2)}, u32[]{:S(2)}) collective-permute-start(bf16[3,7168]{1,0:T(4,128)(2,1)S(1)} %shard_map.74), channel_id=1, source_target_pairs={{0,8},{8,16},{16,24},{24,32},{32,40},{40,48},{48,56},{56,64},{64,7... | collective-permute-start | bytes 129032 | tf_op jit(solution)/shard_map/ppermute | solution.py:444
  10.8 1.2 %collective-permute-done.before = bf16[3,7168]{1,0:T(4,128)(2,1)S(1)} collective-permute-done((bf16[3,7168]{1,0:T(4,128)(2,1)S(1)}, bf16[3,7168]{1,0:T(4,128)(2,1)S(1)}, u32[]{:S(2)}, u32[]{:S(2)}) %collective-permute-start) | collective-permute-done | bytes 43040 | tf_op jit(solution)/shard_map/ppermute | solution.py:444
  11.9 2.5 %all-to-all-done.w = bf16[4,640,128]{2,1,0:T(8,128)(2,1)S(1)} async-done(((bf16[4,640,128]{2,1,0:T(8,128)(2,1)}), bf16[4,640,128]{2,1,0:T(8,128)(2,1)S(1)}, u32[]{:S(2)}, u32[]{:S(2)}) %all-to-all-start) | async-done | bytes 655392 | tf_op jit(solution)/shard_map/all_to_all | solution.py:434
  14.4 8.5 %collective-permute-start.1 = (bf16[4,640,128]{2,1,0:T(8,128)(2,1)S(1)}, bf16[4,640,128]{2,1,0:T(8,128)(2,1)S(1)}, u32[]{:S(2)}, u32[]{:S(2)}) collective-permute-start(bf16[4,640,128]{2,1,0:T(8,128)(2,1)S(1)} %all-to-all-done.w), channel_id=1, source_target_pairs={{0,1},{1,0},{2,3},{3,2},{4,5},{5,4},{6,7},{7,6},{8,9},{9,8},{10,11... | collective-permute-start | bytes 1966088 | tf_op jit(solution)/shard_map/ppermute | solution.py:467
  23.0 0.0 copy-done.3
  23.0 0.0 copy-done.4
  23.0 0.0 copy-start.5
  23.0 1.2 %shard_map.75 = (bf16[2048,256]{1,0:T(8,128)(2,1)S(1)}, f32[64,128]{1,0:T(8,128)S(1)}, bf16[16,5120]{1,0:T(8,128)(2,1)S(1)}) custom-call(f32[64,128]{1,0:T(8,128)S(1)} %bitcast.23, bf16[128,2048]{1,0:T(8,128)(2,1)S(1)} %bitcast.17, bf16[3,7168]{1,0:T(4,128)(2,1)S(1)} %collective-permute-done.before, f32[4,2048]{1,0:T(4,128)S(1)} %copy-done.4), custom_call_target="tpu_custom_call" | custom-call | tf_op jit(solution)/shard_map/pallas_call | solution.py:24
  24.2 0.7 shard_map.76
  24.9 0.0 collective-permute-done.1.w
  24.9 0.0 copy-done.5
  24.9 1.0 shard_map.77
  25.9 21.7 %all_to_all.25.got = s32[4,272,128]{2,1,0:T(8,128)S(1)} all-to-all(s32[4,272,128]{2,1,0:T(8,128)S(1)} %get-tuple-element.29), channel_id=1, replica_groups={{0,8,16,24},{32,40,48,56},{64,72,80,88},{96,104,112,120},{128,136,144,1..., dimensions={0} | all-to-all | bytes 1114112 | tf_op jit(solution)/shard_map/all_to_all | solution.py:427
  47.7 0.3 shard_map.78
  48.0 19.5 %all_to_all.26 = s32[16,1,2176]{2,1,0:T(1,128)S(1)} all-to-all(s32[16,1,2176]{2,1,0:T(1,128)S(1)} %bitcast.22), channel_id=1, replica_groups={{448,320,192,64,480,352,224,96,384,256,128,0,416,288,160,32},{456,328,2..., dimensions={0} | all-to-all | bytes 278528 | tf_op jit(solution)/shard_map/all_to_all | solution.py:427
  67.5 0.2 shard_map.79
  67.7 17.1 %all_to_all.27 = s32[16,1,2176]{2,1,0:T(1,128)S(1)} all-to-all(s32[16,1,2176]{2,1,0:T(1,128)S(1)} %bitcast.21), channel_id=1, replica_groups={{448,320,192,64,480,352,224,96,384,256,128,0,416,288,160,32},{456,328,2..., dimensions={0} | all-to-all | bytes 278528 | tf_op jit(solution)/shard_map/all_to_all | solution.py:427
  84.8 1.2 %shard_map.80 = s32[4,272,128]{2,1,0:T(8,128)} custom-call(s32[272,128]{1,0:T(8,128)S(1)} %bitcast.19, f32[4,512,128]{2,1,0:T(8,128)S(1)} %get-tuple-element.31.prefix, f32[4,16,128]{2,1,0:T(8,128)S(1)} %get-tuple-element.32.decay), custom_call_target="tpu_custom_call" | custom-call | tf_op jit(solution)/shard_map/pallas_call | solution.py:24
  85.9 9.9 %all-to-all-start.4 = ((s32[4,272,128]{2,1,0:T(8,128)}), s32[4,272,128]{2,1,0:T(8,128)S(1)}, u32[]{:S(2)}, u32[]{:S(2)}) async-start(s32[4,272,128]{2,1,0:T(8,128)} %shard_map.80), calls=%async_computation.4 | async-start | bytes 1114112 | tf_op jit(solution)/shard_map/all_to_all | solution.py:427
  96.4 1.3 %shard_map.81 = (f32[2048,128]{1,0:T(8,128)S(1)}, f32[64,128]{1,0:T(8,128)S(1)}) custom-call(s32[1]{0:T(128)} %bitcast.13.accepted, f32[64,128]{1,0:T(8,128)S(1)} %bitcast.24, bf16[128,2048]{1,0:T(8,128)(2,1)S(1)} %bitcast.18, bf16[3,7168]{1,0:T(4,128)(2,1)S(1)} %collective-permute-done.before, f32[4,2048]{1,0:T(4,128)S(1)} %copy-done.4, ...), custom_call_target="tpu_custom_call" | custom-call | tf_op jit(solution)/shard_map/pallas_call | solution.py:24
  97.8 6.3 %all-to-all-done.4.got = s32[4,272,128]{2,1,0:T(8,128)S(1)} async-done(((s32[4,272,128]{2,1,0:T(8,128)}), s32[4,272,128]{2,1,0:T(8,128)S(1)}, u32[]{:S(2)}, u32[]{:S(2)}) %all-to-all-start.4) | async-done | bytes 557088 | tf_op jit(solution)/shard_map/all_to_all | solution.py:427
  104.1 1.1 %shard_map.82 = f32[2048,128]{1,0:T(8,128)} custom-call(s32[4,272,128]{2,1,0:T(8,128)S(1)} %all-to-all-done.4.got, f32[64,128]{1,0:T(8,128)S(1)} %get-tuple-element.35.kept, f32[2048,128]{1,0:T(8,128)S(1)} %get-tuple-element.36.part), custom_call_target="tpu_custom_call" | custom-call | tf_op jit(solution)/shard_map/pallas_call | solution.py:24
  (1 shorter events, 0.0 us)
Async XLA Ops:
  0.0 6.8 %copy-start.1 = (bf16[1,128,2048]{2,1,0:T(8,128)(2,1)S(1)}, bf16[1,128,2048]{2,1,0:T(8,128)(2,1)}, u32[]{:S(2)}) copy-start(bf16[1,128,2048]{2,1,0:T(8,128)(2,1)} %param.8) | copy-start | bytes 1572868
  0.0 6.8 %copy-start = (bf16[1,128,5120]{2,1,0:T(8,128)(2,1)S(1)}, bf16[1,128,5120]{2,1,0:T(8,128)(2,1)}, u32[]{:S(2)}) copy-start(bf16[1,128,5120]{2,1,0:T(8,128)(2,1)} %param.7) | copy-start | bytes 3932164
  0.0 1.1 copy-start.2
  1.9 12.5 %all-to-all-start = ((bf16[4,640,128]{2,1,0:T(8,128)(2,1)}), bf16[4,640,128]{2,1,0:T(8,128)(2,1)S(1)}, u32[]{:S(2)}, u32[]{:S(2)}) async-start(bf16[4,640,128]{2,1,0:T(8,128)(2,1)} %shard_map.73), calls=%async_computation | async-start | bytes 1310720 | tf_op jit(solution)/shard_map/all_to_all | solution.py:434
  6.8 16.2 %copy-start.3 = (f32[1,128,64]{1,2,0:T(8,128)S(1)}, f32[1,128,64]{1,2,0:T(8,128)}, u32[]{:S(2)}) copy-start(f32[1,128,64]{1,2,0:T(8,128)} %param.12) | copy-start | bytes 98308
  6.8 16.2 %copy-start.4 = (f32[4,2048]{1,0:T(4,128)S(1)}, f32[4,2048]{1,0:T(4,128)}, u32[]{:S(2)}) copy-start(f32[4,2048]{1,0:T(4,128)} %taps.5) | copy-start | bytes 98308
  7.1 4.8 %collective-permute-start = (bf16[3,7168]{1,0:T(4,128)(2,1)S(1)}, bf16[3,7168]{1,0:T(4,128)(2,1)S(1)}, u32[]{:S(2)}, u32[]{:S(2)}) collective-permute-start(bf16[3,7168]{1,0:T(4,128)(2,1)S(1)} %shard_map.74), channel_id=1, source_target_pairs={{0,8},{8,16},{16,24},{24,32},{32,40},{40,48},{48,56},{56,64},{64,7... | collective-permute-start | bytes 129032 | tf_op jit(solution)/shard_map/ppermute | solution.py:444
  14.4 10.5 %collective-permute-start.1 = (bf16[4,640,128]{2,1,0:T(8,128)(2,1)S(1)}, bf16[4,640,128]{2,1,0:T(8,128)(2,1)S(1)}, u32[]{:S(2)}, u32[]{:S(2)}) collective-permute-start(bf16[4,640,128]{2,1,0:T(8,128)(2,1)S(1)} %all-to-all-done.w), channel_id=1, source_target_pairs={{0,1},{1,0},{2,3},{3,2},{4,5},{5,4},{6,7},{7,6},{8,9},{9,8},{10,11... | collective-permute-start | bytes 1966088 | tf_op jit(solution)/shard_map/ppermute | solution.py:467
  23.0 1.9 %copy-start.5 = (f32[4,128]{1,0:T(4,128)S(1)}, f32[4,128]{1,0:T(4,128)}, u32[]{:S(2)}) copy-start(f32[4,128]{1,0:T(4,128)} %taps.4) | copy-start | bytes 6148
  85.9 18.2 %all-to-all-start.4 = ((s32[4,272,128]{2,1,0:T(8,128)}), s32[4,272,128]{2,1,0:T(8,128)S(1)}, u32[]{:S(2)}, u32[]{:S(2)}) async-start(s32[4,272,128]{2,1,0:T(8,128)} %shard_map.80), calls=%async_computation.4 | async-start | bytes 1114112 | tf_op jit(solution)/shard_map/all_to_all | solution.py:427

commit v7 on v6

--- a/solution.py
+++ b/solution.py
@@ -126,23 +126,6 @@
         some = tail[:, columns_of(chip, core, depth)]
         edge += jnp.dot(some, w[chip], preferred_element_type=jnp.float32)
     return main, edge
-
-
-def partial_kernel(core, hidden, tail, w, total, rest, held, arrived):
-    chips, depth, size = w.shape
-    moved(
-        [
-            (hidden.at[:, columns_of(chip, side, depth)], to.at[:, pl.ds(chip * depth, depth)])
-            for side, to in ((core[0], held), (1 - core[0], rest))
-            for chip in range(chips)
-        ],
-        arrived,
-    )
-    main = jnp.zeros((hidden.shape[0], size), jnp.float32)
-    edge = jnp.zeros((tail.shape[0], size), jnp.float32)
-    main, edge = project(core[0], held, tail, w, main, edge)
-    total[0:ROWS, :] = edge
-    total[ROWS:, :] = main
 
 
 def split_lanes(wide):
@@ -194,8 +177,38 @@
 
 
 def inputs_kernel(
-    steps, values, before, taps, ends, end_logs, tail, extended, held, steps_held, taps_held, arrived
+    core,
+    hidden,
+    w,
+    steps,
+    values,
+    before,
+    taps,
+    ends,
+    end_logs,
+    tail,
+    total,
+    rest,
+    extended,
+    held,
+    steps_held,
+    taps_held,
+    arrived,
+    columns,
+    landed,
 ):
+    chips, depth, size = w.shape
+    moves = [
+        pltpu.make_async_copy(
+            hidden.at[:, columns_of(chip, side, depth)],
+            to.at[:, pl.ds(chip * depth, depth)],
+            landed.at[i * chips + chip],
+        )
+        for i, (side, to) in enumerate(((core[0], columns), (1 - core[0], rest)))
+        for chip in range(chips)
+    ]
+    for move in moves:
+        move.start()
     moved([(values, held), (steps, steps_held), (taps, taps_held)], arrived)
     margin = taps.shape[0] - 1
     width = tail.shape[1]
@@ -211,6 +224,13 @@
         rows = mixed.shape[0]
         some = weight[part * heads : (part + 1) * heads, :]
         ends[part * rows : (part + 1) * rows, :] = weighted(mixed, some)
+    for move in moves:
+        move.wait()
+    main = jnp.zeros((hidden.shape[0], size), jnp.float32)
+    edge = jnp.zeros((tail.shape[0], size), jnp.float32)
+    main, edge = project(core[0], columns, tail, w, main, edge)
+    total[0:ROWS, :] = edge
+    total[ROWS:, :] = main
 
 
 def right_side(mixed_b):
@@ -452,28 +472,26 @@
         pltpu.VMEM(conv_x.shape, f32),
         dma((3,)),
     ]
-    ends_x, end_logs, tail = call(
+    w_own, before, core, wraps = lax.optimization_barrier((w_own, before, core, wraps))
+    w_other = lax.ppermute(w_own, "fsdp", [(i, i ^ 1) for i in range(parts)])
+    ends_x, end_logs, tail, begun, rest = call(
         inputs_kernel,
+        core,
+        tokens,
+        w_own,
         steps,
         values,
         before,
         conv_x,
-        far=(0, 1, 3),
-        out=[array((channels, 2 * length), bf16), wide, array((ROWS, width), bf16)],
-        scratch=scratch,
-    )
-
-    w_own, before, core, wraps = lax.optimization_barrier((w_own, before, core, wraps))
-    w_other = lax.ppermute(w_own, "fsdp", [(i, i ^ 1) for i in range(parts)])
-    begun, rest = call(
-        partial_kernel,
-        core,
-        tokens,
-        tail,
-        w_own,
-        far=(1,),
-        out=[array((ROWS + length, size), f32), array((length, width // 2), bf16)],
-        scratch=[pltpu.VMEM((length, width // 2), bf16), dma((parts,))],
+        far=(1, 3, 4, 6),
+        out=[
+            array((channels, 2 * length), bf16),
+            wide,
+            array((ROWS, width), bf16),
+            array((ROWS + length, size), f32),
+            array((length, width // 2), bf16),
+        ],
+        scratch=scratch + [pltpu.VMEM((length, width // 2), bf16), dma((parts,))],
     )
 
     slices = array((GROUP, heads * message, size), i32)

time: 106 us -> 106 us (level)
    pallas_call x9 -> x8, Pallas kernels: 7.33 us -> 7.33 us  [call(): pl.pallas_call(kernel, in_specs=[pl.BlockSpec(memory_space=place) for pla...]
where the time goes in v7:
time: 106 us; the launch traced here: 105 us
  blocking collectives  58.3 us (55%)
  starting transfers between devices  26.8 us (25%)
  waiting for transfers between devices  9.99 us (9%)
  Pallas kernels  8.19 us (8%)
  local copies, waits for them, and re-layouts  1.07 us (1%)
    all_to_all x3, blocking collectives, exchange(): lax.all_to_all(sent, ('seq', 'fsdp'), 0, 0, axis_index_groups=members)  58.3 us
    all_to_all x1, starting transfers between devices, exchange(): lax.all_to_all(sent, ('seq', 'fsdp'), 0, 0, axis_index_groups=members)  9.85 us
    ppermute x1, starting transfers between devices, on_device(): w_other = lax.ppermute(w_own, 'fsdp', [(i, i ^ 1) for i in range(parts)])  8.54 us
    pallas_call x8, Pallas kernels, call(): pl.pallas_call(kernel, in_specs=[pl.BlockSpec(memory_space=place) for pla...  7.33 us
    all_to_all x1, waiting for transfers between devices, exchange(): lax.all_to_all(sent, ('seq', 'fsdp'), 0, 0, axis_index_groups=members)  6.32 us
    all_to_all x1, starting transfers between devices, on_device(): w_own = lax.all_to_all(w_copies, 'fsdp', 0, 0, axis_index_groups=chips)  4.85 us
    ppermute x1, starting transfers between devices, on_device(): before = lax.ppermute(edge, 'seq', [(i, i + 1) for i in range(shards - 1)])  3.54 us
    all_to_all x1, waiting for transfers between devices, on_device(): w_own = lax.all_to_all(w_copies, 'fsdp', 0, 0, axis_index_groups=chips)  2.48 us
  transfers between devices with their start and end apart: 4, of which 3 were waited for; matrix products, arithmetic and copies ran while one was open for 0% of the time, Pallas kernels for 3%

profile of v7, /device:TPU:1, one launch (start us, length us, event | category | flops | bytes accessed | tf_op | source)
XLA Modules:
  0.0 105.1 jit_solution(6620057940262159304)
XLA Ops:
  0.0 0.0 copy-start
  0.0 0.0 copy-start.1
  0.0 0.0 copy-start.2
  0.0 1.0 copy-done.2
  1.1 0.9 shard_map.73
  1.9 4.9 %all-to-all-start = ((bf16[4,640,128]{2,1,0:T(8,128)(2,1)}), bf16[4,640,128]{2,1,0:T(8,128)(2,1)S(1)}, u32[]{:S(2)}, u32[]{:S(2)}) async-start(bf16[4,640,128]{2,1,0:T(8,128)(2,1)} %shard_map.73), calls=%async_computation | async-start | bytes 1310720 | tf_op jit(solution)/shard_map/all_to_all | solution.py:454
  6.8 0.0 copy-start.3
  6.8 0.0 copy-start.4
  6.8 0.0 copy-done
  6.8 0.0 copy-done.1
  6.8 0.3 shard_map.74
  7.1 3.5 %collective-permute-start = (bf16[3,7168]{1,0:T(4,128)(2,1)S(1)}, bf16[3,7168]{1,0:T(4,128)(2,1)S(1)}, u32[]{:S(2)}, u32[]{:S(2)}) collective-permute-start(bf16[3,7168]{1,0:T(4,128)(2,1)S(1)} %shard_map.74), channel_id=1, source_target_pairs={{0,8},{8,16},{16,24},{24,32},{32,40},{40,48},{48,56},{56,64},{64,7... | collective-permute-start | bytes 129032 | tf_op jit(solution)/shard_map/ppermute | solution.py:464
  10.8 1.2 %collective-permute-done.before = bf16[3,7168]{1,0:T(4,128)(2,1)S(1)} collective-permute-done((bf16[3,7168]{1,0:T(4,128)(2,1)S(1)}, bf16[3,7168]{1,0:T(4,128)(2,1)S(1)}, u32[]{:S(2)}, u32[]{:S(2)}) %collective-permute-start) | collective-permute-done | bytes 43040 | tf_op jit(solution)/shard_map/ppermute | solution.py:464
  11.9 2.5 %all-to-all-done.w = bf16[4,640,128]{2,1,0:T(8,128)(2,1)S(1)} async-done(((bf16[4,640,128]{2,1,0:T(8,128)(2,1)}), bf16[4,640,128]{2,1,0:T(8,128)(2,1)S(1)}, u32[]{:S(2)}, u32[]{:S(2)}) %all-to-all-start) | async-done | bytes 655392 | tf_op jit(solution)/shard_map/all_to_all | solution.py:454
  14.4 8.5 %collective-permute-start.1 = (bf16[4,640,128]{2,1,0:T(8,128)(2,1)S(1)}, bf16[4,640,128]{2,1,0:T(8,128)(2,1)S(1)}, u32[]{:S(2)}, u32[]{:S(2)}) collective-permute-start(bf16[4,640,128]{2,1,0:T(8,128)(2,1)S(1)} %all-to-all-done.w), channel_id=1, source_target_pairs={{0,1},{1,0},{2,3},{3,2},{4,5},{5,4},{6,7},{7,6},{8,9},{9,8},{10,11... | collective-permute-start | bytes 1966088 | tf_op jit(solution)/shard_map/ppermute | solution.py:476
  23.0 0.0 copy-done.3
  23.0 0.0 copy-done.4
  23.0 0.0 copy-start.5
  23.0 1.9 %shard_map.75 = (bf16[2048,256]{1,0:T(8,128)(2,1)S(1)}, f32[64,128]{1,0:T(8,128)S(1)}, bf16[16,5120]{1,0:T(8,128)(2,1)S(1)}, f32[144,128]{1,0:T(8,128)S(1)}, bf16[128,2560]{1,0:T(8,128)(2,1)S(1)}) custom-call(s32[1]{0:T(128)} %bitcast.2.core, bf16[128,5120]{1,0:T(8,128)(2,1)S(1)} %bitcast.15, bf16[4,640,128]{2,1,0:T(8,128)(2,1)S(1)} %all-to-all-done.w, ...), custom_call_target="tpu_custom_call" | custom-call | tf_op jit(solution)/shard_map/pallas_call | solution.py:24
  24.9 0.0 collective-permute-done.1.w
  24.9 0.0 copy-done.5
  24.9 1.0 shard_map.76
  25.9 21.7 %all_to_all.25.got = s32[4,272,128]{2,1,0:T(8,128)S(1)} all-to-all(s32[4,272,128]{2,1,0:T(8,128)S(1)} %get-tuple-element.30), channel_id=1, replica_groups={{0,8,16,24},{32,40,48,56},{64,72,80,88},{96,104,112,120},{128,136,144,1..., dimensions={0} | all-to-all | bytes 1114112 | tf_op jit(solution)/shard_map/all_to_all | solution.py:447
  47.7 0.3 shard_map.77
  48.0 19.5 %all_to_all.26 = s32[16,1,2176]{2,1,0:T(1,128)S(1)} all-to-all(s32[16,1,2176]{2,1,0:T(1,128)S(1)} %bitcast.22), channel_id=1, replica_groups={{448,320,192,64,480,352,224,96,384,256,128,0,416,288,160,32},{456,328,2..., dimensions={0} | all-to-all | bytes 278528 | tf_op jit(solution)/shard_map/all_to_all | solution.py:447
  67.5 0.2 shard_map.78
  67.7 17.1 %all_to_all.27 = s32[16,1,2176]{2,1,0:T(1,128)S(1)} all-to-all(s32[16,1,2176]{2,1,0:T(1,128)S(1)} %bitcast.21), channel_id=1, replica_groups={{448,320,192,64,480,352,224,96,384,256,128,0,416,288,160,32},{456,328,2..., dimensions={0} | all-to-all | bytes 278528 | tf_op jit(solution)/shard_map/all_to_all | solution.py:447
  84.7 1.2 %shard_map.79 = s32[4,272,128]{2,1,0:T(8,128)} custom-call(s32[272,128]{1,0:T(8,128)S(1)} %bitcast.19, f32[4,512,128]{2,1,0:T(8,128)S(1)} %get-tuple-element.32.prefix, f32[4,16,128]{2,1,0:T(8,128)S(1)} %get-tuple-element.33.decay), custom_call_target="tpu_custom_call" | custom-call | tf_op jit(solution)/shard_map/pallas_call | solution.py:24
  85.9 9.9 %all-to-all-start.4 = ((s32[4,272,128]{2,1,0:T(8,128)}), s32[4,272,128]{2,1,0:T(8,128)S(1)}, u32[]{:S(2)}, u32[]{:S(2)}) async-start(s32[4,272,128]{2,1,0:T(8,128)} %shard_map.79), calls=%async_computation.4 | async-start | bytes 1114112 | tf_op jit(solution)/shard_map/all_to_all | solution.py:447
  96.4 1.3 %shard_map.80 = (f32[2048,128]{1,0:T(8,128)S(1)}, f32[64,128]{1,0:T(8,128)S(1)}) custom-call(s32[1]{0:T(128)} %bitcast.13.accepted, f32[64,128]{1,0:T(8,128)S(1)} %bitcast.24, bf16[128,2048]{1,0:T(8,128)(2,1)S(1)} %bitcast.18, bf16[3,7168]{1,0:T(4,128)(2,1)S(1)} %collective-permute-done.before, f32[4,2048]{1,0:T(4,128)S(1)} %copy-done.4, ...), custom_call_target="tpu_custom_call" | custom-call | tf_op jit(solution)/shard_map/pallas_call | solution.py:24
  97.7 6.3 %all-to-all-done.4.got = s32[4,272,128]{2,1,0:T(8,128)S(1)} async-done(((s32[4,272,128]{2,1,0:T(8,128)}), s32[4,272,128]{2,1,0:T(8,128)S(1)}, u32[]{:S(2)}, u32[]{:S(2)}) %all-to-all-start.4) | async-done | bytes 557088 | tf_op jit(solution)/shard_map/all_to_all | solution.py:447
  104.1 1.1 %shard_map.81 = f32[2048,128]{1,0:T(8,128)} custom-call(s32[4,272,128]{2,1,0:T(8,128)S(1)} %all-to-all-done.4.got, f32[64,128]{1,0:T(8,128)S(1)} %get-tuple-element.35.kept, f32[2048,128]{1,0:T(8,128)S(1)} %get-tuple-element.36.part), custom_call_target="tpu_custom_call" | custom-call | tf_op jit(solution)/shard_map/pallas_call | solution.py:24
Async XLA Ops:
  0.0 6.8 %copy-start = (bf16[1,128,5120]{2,1,0:T(8,128)(2,1)S(1)}, bf16[1,128,5120]{2,1,0:T(8,128)(2,1)}, u32[]{:S(2)}) copy-start(bf16[1,128,5120]{2,1,0:T(8,128)(2,1)} %param.7) | copy-start | bytes 3932164
  0.0 6.8 %copy-start.1 = (bf16[1,128,2048]{2,1,0:T(8,128)(2,1)S(1)}, bf16[1,128,2048]{2,1,0:T(8,128)(2,1)}, u32[]{:S(2)}) copy-start(bf16[1,128,2048]{2,1,0:T(8,128)(2,1)} %param.8) | copy-start | bytes 1572868
  0.0 1.1 copy-start.2
  1.9 12.5 %all-to-all-start = ((bf16[4,640,128]{2,1,0:T(8,128)(2,1)}), bf16[4,640,128]{2,1,0:T(8,128)(2,1)S(1)}, u32[]{:S(2)}, u32[]{:S(2)}) async-start(bf16[4,640,128]{2,1,0:T(8,128)(2,1)} %shard_map.73), calls=%async_computation | async-start | bytes 1310720 | tf_op jit(solution)/shard_map/all_to_all | solution.py:454
  6.8 16.2 %copy-start.3 = (f32[1,128,64]{1,2,0:T(8,128)S(1)}, f32[1,128,64]{1,2,0:T(8,128)}, u32[]{:S(2)}) copy-start(f32[1,128,64]{1,2,0:T(8,128)} %param.12) | copy-start | bytes 98308
  6.8 16.2 %copy-start.4 = (f32[4,2048]{1,0:T(4,128)S(1)}, f32[4,2048]{1,0:T(4,128)}, u32[]{:S(2)}) copy-start(f32[4,2048]{1,0:T(4,128)} %taps.5) | copy-start | bytes 98308
  7.1 4.8 %collective-permute-start = (bf16[3,7168]{1,0:T(4,128)(2,1)S(1)}, bf16[3,7168]{1,0:T(4,128)(2,1)S(1)}, u32[]{:S(2)}, u32[]{:S(2)}) collective-permute-start(bf16[3,7168]{1,0:T(4,128)(2,1)S(1)} %shard_map.74), channel_id=1, source_target_pairs={{0,8},{8,16},{16,24},{24,32},{32,40},{40,48},{48,56},{56,64},{64,7... | collective-permute-start | bytes 129032 | tf_op jit(solution)/shard_map/ppermute | solution.py:464
  14.4 10.5 %collective-permute-start.1 = (bf16[4,640,128]{2,1,0:T(8,128)(2,1)S(1)}, bf16[4,640,128]{2,1,0:T(8,128)(2,1)S(1)}, u32[]{:S(2)}, u32[]{:S(2)}) collective-permute-start(bf16[4,640,128]{2,1,0:T(8,128)(2,1)S(1)} %all-to-all-done.w), channel_id=1, source_target_pairs={{0,1},{1,0},{2,3},{3,2},{4,5},{5,4},{6,7},{7,6},{8,9},{9,8},{10,11... | collective-permute-start | bytes 1966088 | tf_op jit(solution)/shard_map/ppermute | solution.py:476
  23.0 1.9 %copy-start.5 = (f32[4,128]{1,0:T(4,128)S(1)}, f32[4,128]{1,0:T(4,128)}, u32[]{:S(2)}) copy-start(f32[4,128]{1,0:T(4,128)} %taps.4) | copy-start | bytes 6148
  85.9 18.2 %all-to-all-start.4 = ((s32[4,272,128]{2,1,0:T(8,128)}), s32[4,272,128]{2,1,0:T(8,128)S(1)}, u32[]{:S(2)}, u32[]{:S(2)}) async-start(s32[4,272,128]{2,1,0:T(8,128)} %shard_map.79), calls=%async_computation.4 | async-start | bytes 1114112 | tf_op jit(solution)/shard_map/all_to_all | solution.py:447

commit v8 on v6

--- a/solution.py
+++ b/solution.py
@@ -368,18 +368,22 @@
 
 
 def final_kernel(headdim, got, kept, part, out, staged, arrived):
-    rows = part.shape[0] // GROUP
+    words = headdim // 2
+    heads = got.shape[1] // (words + 1)
+    few = heads // 2
     size = part.shape[1]
-    heads = rows // headdim
     moves = []
-    for owner in range(GROUP):
-        state, _ = read_slice(got.at[owner], headdim)
-        scaled = kept[owner * heads : (owner + 1) * heads, :][:, None, :] * state
-        lines = slice(owner * rows, (owner + 1) * rows)
-        staged[lines, :] = scaled.reshape(rows, size) + part[lines, :]
-        lines = pl.ds(owner * rows, rows)
+    for piece in range(2 * GROUP):
+        owner, first = piece // 2, piece % 2 * few
+        notes = got[owner, heads * words + first : heads * words + first + few, :]
+        coded = got[owner, first * words : (first + few) * words, :].reshape(few, words, size)
+        factor = down(high_of(notes).astype(jnp.float32)) * kept[piece * few : (piece + 1) * few, :]
+        rows = few * headdim
+        lines = slice(piece * rows, (piece + 1) * rows)
+        staged[lines, :] = (codes_of(coded) * factor[:, None, :]).reshape(rows, size) + part[lines, :]
+        lines = pl.ds(piece * rows, rows)
         moves.append(
-            pltpu.make_async_copy(staged.at[lines, :], out.at[lines, :], arrived.at[owner])
+            pltpu.make_async_copy(staged.at[lines, :], out.at[lines, :], arrived.at[piece])
         )
         moves[-1].start()
     for move in moves:
@@ -542,7 +546,7 @@
         part,
         out=array((channels, size), f32),
         out_space=pltpu.HBM,
-        scratch=[pltpu.VMEM((channels, size), f32), dma((GROUP,))],
+        scratch=[pltpu.VMEM((channels, size), f32), dma((2 * GROUP,))],
     )
     return final.reshape(1, 1, head_count, headdim, size)
 

time: 106 us -> 106 us (level)
  no operation moved by 1% of the time
where the time goes in v8:
time: 106 us; the launch traced here: 105 us
  blocking collectives  58.3 us (55%)
  starting transfers between devices  26.8 us (25%)
  waiting for transfers between devices  9.99 us (9%)
  Pallas kernels  8.18 us (8%)
  local copies, waits for them, and re-layouts  1.07 us (1%)
    all_to_all x3, blocking collectives, exchange(): lax.all_to_all(sent, ('seq', 'fsdp'), 0, 0, axis_index_groups=members)  58.3 us
    all_to_all x1, starting transfers between devices, exchange(): lax.all_to_all(sent, ('seq', 'fsdp'), 0, 0, axis_index_groups=members)  9.85 us
    ppermute x1, starting transfers between devices, on_device(): w_other = lax.ppermute(w_own, 'fsdp', [(i, i ^ 1) for i in range(parts)])  8.54 us
    pallas_call x9, Pallas kernels, call(): pl.pallas_call(kernel, in_specs=[pl.BlockSpec(memory_space=place) for pla...  7.32 us
    all_to_all x1, waiting for transfers between devices, exchange(): lax.all_to_all(sent, ('seq', 'fsdp'), 0, 0, axis_index_groups=members)  6.32 us
    all_to_all x1, starting transfers between devices, on_device(): w_own = lax.all_to_all(w_copies, 'fsdp', 0, 0, axis_index_groups=chips)  4.85 us
    ppermute x1, starting transfers between devices, on_device(): before = lax.ppermute(edge, 'seq', [(i, i + 1) for i in range(shards - 1)])  3.54 us
    all_to_all x1, waiting for transfers between devices, on_device(): w_own = lax.all_to_all(w_copies, 'fsdp', 0, 0, axis_index_groups=chips)  2.48 us
  transfers between devices with their start and end apart: 4, of which 3 were waited for; matrix products, arithmetic and copies ran while one was open for 0% of the time, Pallas kernels for 3%

profile of v8, /device:TPU:1, one launch (start us, length us, event | category | flops | bytes accessed | tf_op | source)
XLA Modules:
  0.0 105.1 jit_solution(9216543683093885338)
XLA Ops:
  0.0 0.0 copy-start.1
  0.0 0.0 copy-start
  0.0 1.0 copy-done.2
  1.1 0.9 shard_map.73
  1.9 4.9 %all-to-all-start = ((bf16[4,640,128]{2,1,0:T(8,128)(2,1)}), bf16[4,640,128]{2,1,0:T(8,128)(2,1)S(1)}, u32[]{:S(2)}, u32[]{:S(2)}) async-start(bf16[4,640,128]{2,1,0:T(8,128)(2,1)} %shard_map.73), calls=%async_computation | async-start | bytes 1310720 | tf_op jit(solution)/shard_map/all_to_all | solution.py:438
  6.8 0.0 copy-start.3
  6.8 0.0 copy-start.4
  6.8 0.0 copy-done.1
  6.8 0.0 copy-done
  6.8 0.3 shard_map.74
  7.1 3.5 %collective-permute-start = (bf16[3,7168]{1,0:T(4,128)(2,1)S(1)}, bf16[3,7168]{1,0:T(4,128)(2,1)S(1)}, u32[]{:S(2)}, u32[]{:S(2)}) collective-permute-start(bf16[3,7168]{1,0:T(4,128)(2,1)S(1)} %shard_map.74), channel_id=1, source_target_pairs={{0,8},{8,16},{16,24},{24,32},{32,40},{40,48},{48,56},{56,64},{64,7... | collective-permute-start | bytes 129032 | tf_op jit(solution)/shard_map/ppermute | solution.py:448
  10.8 1.2 %collective-permute-done.before = bf16[3,7168]{1,0:T(4,128)(2,1)S(1)} collective-permute-done((bf16[3,7168]{1,0:T(4,128)(2,1)S(1)}, bf16[3,7168]{1,0:T(4,128)(2,1)S(1)}, u32[]{:S(2)}, u32[]{:S(2)}) %collective-permute-start) | collective-permute-done | bytes 43040 | tf_op jit(solution)/shard_map/ppermute | solution.py:448
  11.9 2.5 %all-to-all-done.w = bf16[4,640,128]{2,1,0:T(8,128)(2,1)S(1)} async-done(((bf16[4,640,128]{2,1,0:T(8,128)(2,1)}), bf16[4,640,128]{2,1,0:T(8,128)(2,1)S(1)}, u32[]{:S(2)}, u32[]{:S(2)}) %all-to-all-start) | async-done | bytes 655392 | tf_op jit(solution)/shard_map/all_to_all | solution.py:438
  14.4 8.5 %collective-permute-start.1 = (bf16[4,640,128]{2,1,0:T(8,128)(2,1)S(1)}, bf16[4,640,128]{2,1,0:T(8,128)(2,1)S(1)}, u32[]{:S(2)}, u32[]{:S(2)}) collective-permute-start(bf16[4,640,128]{2,1,0:T(8,128)(2,1)S(1)} %all-to-all-done.w), channel_id=1, source_target_pairs={{0,1},{1,0},{2,3},{3,2},{4,5},{5,4},{6,7},{7,6},{8,9},{9,8},{10,11... | collective-permute-start | bytes 1966088 | tf_op jit(solution)/shard_map/ppermute | solution.py:471
  23.0 0.0 copy-done.3
  23.0 0.0 copy-done.4
  23.0 0.0 copy-start.5
  23.0 1.2 %shard_map.75 = (bf16[2048,256]{1,0:T(8,128)(2,1)S(1)}, f32[64,128]{1,0:T(8,128)S(1)}, bf16[16,5120]{1,0:T(8,128)(2,1)S(1)}) custom-call(f32[64,128]{1,0:T(8,128)S(1)} %bitcast.23, bf16[128,2048]{1,0:T(8,128)(2,1)S(1)} %bitcast.17, bf16[3,7168]{1,0:T(4,128)(2,1)S(1)} %collective-permute-done.before, f32[4,2048]{1,0:T(4,128)S(1)} %copy-done.4), custom_call_target="tpu_custom_call" | custom-call | tf_op jit(solution)/shard_map/pallas_call | solution.py:24
  24.2 0.7 shard_map.76
  24.9 0.0 collective-permute-done.1.w
  24.9 0.0 copy-done.5
  24.9 1.0 shard_map.77
  25.9 21.7 %all_to_all.25.got = s32[4,272,128]{2,1,0:T(8,128)S(1)} all-to-all(s32[4,272,128]{2,1,0:T(8,128)S(1)} %get-tuple-element.29), channel_id=1, replica_groups={{0,8,16,24},{32,40,48,56},{64,72,80,88},{96,104,112,120},{128,136,144,1..., dimensions={0} | all-to-all | bytes 1114112 | tf_op jit(solution)/shard_map/all_to_all | solution.py:431
  47.7 0.3 shard_map.78
  48.0 19.5 %all_to_all.26 = s32[16,1,2176]{2,1,0:T(1,128)S(1)} all-to-all(s32[16,1,2176]{2,1,0:T(1,128)S(1)} %bitcast.22), channel_id=1, replica_groups={{448,320,192,64,480,352,224,96,384,256,128,0,416,288,160,32},{456,328,2..., dimensions={0} | all-to-all | bytes 278528 | tf_op jit(solution)/shard_map/all_to_all | solution.py:431
  67.5 0.2 shard_map.79
  67.7 17.1 %all_to_all.27 = s32[16,1,2176]{2,1,0:T(1,128)S(1)} all-to-all(s32[16,1,2176]{2,1,0:T(1,128)S(1)} %bitcast.21), channel_id=1, replica_groups={{448,320,192,64,480,352,224,96,384,256,128,0,416,288,160,32},{456,328,2..., dimensions={0} | all-to-all | bytes 278528 | tf_op jit(solution)/shard_map/all_to_all | solution.py:431
  84.8 1.2 %shard_map.80 = s32[4,272,128]{2,1,0:T(8,128)} custom-call(s32[272,128]{1,0:T(8,128)S(1)} %bitcast.19, f32[4,512,128]{2,1,0:T(8,128)S(1)} %get-tuple-element.31.prefix, f32[4,16,128]{2,1,0:T(8,128)S(1)} %get-tuple-element.32.decay), custom_call_target="tpu_custom_call" | custom-call | tf_op jit(solution)/shard_map/pallas_call | solution.py:24
  85.9 9.9 %all-to-all-start.4 = ((s32[4,272,128]{2,1,0:T(8,128)}), s32[4,272,128]{2,1,0:T(8,128)S(1)}, u32[]{:S(2)}, u32[]{:S(2)}) async-start(s32[4,272,128]{2,1,0:T(8,128)} %shard_map.80), calls=%async_computation.4 | async-start | bytes 1114112 | tf_op jit(solution)/shard_map/all_to_all | solution.py:431
  96.4 1.3 %shard_map.81 = (f32[2048,128]{1,0:T(8,128)S(1)}, f32[64,128]{1,0:T(8,128)S(1)}) custom-call(s32[1]{0:T(128)} %bitcast.13.accepted, f32[64,128]{1,0:T(8,128)S(1)} %bitcast.24, bf16[128,2048]{1,0:T(8,128)(2,1)S(1)} %bitcast.18, bf16[3,7168]{1,0:T(4,128)(2,1)S(1)} %collective-permute-done.before, f32[4,2048]{1,0:T(4,128)S(1)} %copy-done.4, ...), custom_call_target="tpu_custom_call" | custom-call | tf_op jit(solution)/shard_map/pallas_call | solution.py:24
  97.8 6.3 %all-to-all-done.4.got = s32[4,272,128]{2,1,0:T(8,128)S(1)} async-done(((s32[4,272,128]{2,1,0:T(8,128)}), s32[4,272,128]{2,1,0:T(8,128)S(1)}, u32[]{:S(2)}, u32[]{:S(2)}) %all-to-all-start.4) | async-done | bytes 557088 | tf_op jit(solution)/shard_map/all_to_all | solution.py:431
  104.1 1.1 %shard_map.82 = f32[2048,128]{1,0:T(8,128)} custom-call(s32[4,272,128]{2,1,0:T(8,128)S(1)} %all-to-all-done.4.got, f32[64,128]{1,0:T(8,128)S(1)} %get-tuple-element.35.kept, f32[2048,128]{1,0:T(8,128)S(1)} %get-tuple-element.36.part), custom_call_target="tpu_custom_call" | custom-call | tf_op jit(solution)/shard_map/pallas_call | solution.py:24
  (1 shorter events, 0.0 us)
Async XLA Ops:
  0.0 6.8 %copy-start.1 = (bf16[1,128,2048]{2,1,0:T(8,128)(2,1)S(1)}, bf16[1,128,2048]{2,1,0:T(8,128)(2,1)}, u32[]{:S(2)}) copy-start(bf16[1,128,2048]{2,1,0:T(8,128)(2,1)} %param.8) | copy-start | bytes 1572868
  0.0 6.8 %copy-start = (bf16[1,128,5120]{2,1,0:T(8,128)(2,1)S(1)}, bf16[1,128,5120]{2,1,0:T(8,128)(2,1)}, u32[]{:S(2)}) copy-start(bf16[1,128,5120]{2,1,0:T(8,128)(2,1)} %param.7) | copy-start | bytes 3932164
  0.0 1.1 copy-start.2
  1.9 12.5 %all-to-all-start = ((bf16[4,640,128]{2,1,0:T(8,128)(2,1)}), bf16[4,640,128]{2,1,0:T(8,128)(2,1)S(1)}, u32[]{:S(2)}, u32[]{:S(2)}) async-start(bf16[4,640,128]{2,1,0:T(8,128)(2,1)} %shard_map.73), calls=%async_computation | async-start | bytes 1310720 | tf_op jit(solution)/shard_map/all_to_all | solution.py:438
  6.8 16.2 %copy-start.3 = (f32[1,128,64]{1,2,0:T(8,128)S(1)}, f32[1,128,64]{1,2,0:T(8,128)}, u32[]{:S(2)}) copy-start(f32[1,128,64]{1,2,0:T(8,128)} %param.12) | copy-start | bytes 98308
  6.8 16.2 %copy-start.4 = (f32[4,2048]{1,0:T(4,128)S(1)}, f32[4,2048]{1,0:T(4,128)}, u32[]{:S(2)}) copy-start(f32[4,2048]{1,0:T(4,128)} %taps.5) | copy-start | bytes 98308
  7.1 4.8 %collective-permute-start = (bf16[3,7168]{1,0:T(4,128)(2,1)S(1)}, bf16[3,7168]{1,0:T(4,128)(2,1)S(1)}, u32[]{:S(2)}, u32[]{:S(2)}) collective-permute-start(bf16[3,7168]{1,0:T(4,128)(2,1)S(1)} %shard_map.74), channel_id=1, source_target_pairs={{0,8},{8,16},{16,24},{24,32},{32,40},{40,48},{48,56},{56,64},{64,7... | collective-permute-start | bytes 129032 | tf_op jit(solution)/shard_map/ppermute | solution.py:448
  14.4 10.5 %collective-permute-start.1 = (bf16[4,640,128]{2,1,0:T(8,128)(2,1)S(1)}, bf16[4,640,128]{2,1,0:T(8,128)(2,1)S(1)}, u32[]{:S(2)}, u32[]{:S(2)}) collective-permute-start(bf16[4,640,128]{2,1,0:T(8,128)(2,1)S(1)} %all-to-all-done.w), channel_id=1, source_target_pairs={{0,1},{1,0},{2,3},{3,2},{4,5},{5,4},{6,7},{7,6},{8,9},{9,8},{10,11... | collective-permute-start | bytes 1966088 | tf_op jit(solution)/shard_map/ppermute | solution.py:471
  23.0 1.9 %copy-start.5 = (f32[4,128]{1,0:T(4,128)S(1)}, f32[4,128]{1,0:T(4,128)}, u32[]{:S(2)}) copy-start(f32[4,128]{1,0:T(4,128)} %taps.4) | copy-start | bytes 6148
  85.9 18.2 %all-to-all-start.4 = ((s32[4,272,128]{2,1,0:T(8,128)}), s32[4,272,128]{2,1,0:T(8,128)S(1)}, u32[]{:S(2)}, u32[]{:S(2)}) async-start(s32[4,272,128]{2,1,0:T(8,128)} %shard_map.80), calls=%async_computation.4 | async-start | bytes 1114112 | tf_op jit(solution)/shard_map/all_to_all | solution.py:431
